TPU v7x, 256 devices: a whole 4x4x8 slice. The times are simulated.
256 devices in a mesh: replica: 8 (over z_lo, y), fsdp: 32 (over x, z_hi, core).
Axes of the slice: x: 4, y: 4, z: 8 (z_hi: 4, z_lo: 2; z = z_hi * 2 + z_lo), core: 2. Of those that a mesh axis runs over, the one named last changes fastest.
Arguments:
- tokens: bfloat16 [8, 4096, 6144], P('replica', 'fsdp'), may hold values from -6 to 6
- grad_out: bfloat16 [8, 4096, 6144], P('replica', 'fsdp'), may hold values from -6 to 6
- expert_ids: int32 [8, 4096, 2], P('replica', 'fsdp'), may hold values from 0 to 7, as said below
- gate_share: float32 [8, 4096], P('replica', 'fsdp'), may hold values from 0.05 to 0.95
- up_weight: bfloat16 [8, 6144, 8192], P('replica', None, 'fsdp'), may hold values from -0.078125 to 0.078125
- down_weight: bfloat16 [8, 8192, 6144], P('replica', 'fsdp'), may hold values from -0.0625 to 0.0625
- local_keys: float32 [8, 6144, 512], P('replica', 'fsdp'), may hold values from -6 to 6
- outer_keys: float32 [6144, 512], P('fsdp'), may hold values from -6 to 6
- momentum: float32 [6144, 512], P('fsdp', 'replica'), may hold values from -4 to 4
Outputs:
- input_grad: bfloat16 [8, 4096, 6144], P('replica', 'fsdp')
- new_outer: float32 [6144, 512], P('fsdp')
- new_momentum: float32 [6144, 512], P('fsdp', 'replica')
- outer_copy: bfloat16 [6144, 512], P('fsdp')
Inputs may be any that keep to these rules, and one draw needn't show every extreme that they name: `expert_ids`: every token names two different experts. In each replica, each device's 128 consecutive tokens hold exactly 16 that name expert 0.
All inputs are finite; a program needn't handle non-finite values.
Results may differ from a plain program's by a relative error of at most 0.0049.
Values may be sent and summed in bfloat16 or wider, within the bound.
No kernel may reach another device: no remote copies, remote signals or barrier semaphores. Data moves between devices by JAX's collectives and lax.ppermute only.
A program may use at most 128 MiB of HBM per device.

v0:
```python
import functools

import jax
import jax.numpy as jnp
from jax import lax
from jax.experimental import pallas as pl
from jax.experimental.pallas import tpu as pltpu
from jax.sharding import Mesh
from jax.sharding import PartitionSpec as P

CAP = 16
OUTER_BETA = 0.9
OUTER_RATE = 0.7
MIB = 1 << 20
F32, BF16 = jnp.float32, jnp.bfloat16


def hop(value, axis, step):
    size = lax.axis_size(axis)
    return lax.ppermute(value, axis, [(i, (i + step) % size) for i in range(size)])


def mirrored(value, axis, step):
    size = lax.axis_size(axis)
    pairs = []
    for i in range(size):
        pairs.append((2 * i, 2 * ((i + step) % size)))
        pairs.append((2 * i + 1, 2 * ((i - step) % size) + 1))
    return lax.ppermute(value, (axis, "core"), pairs)


def after(value, *earlier):
    return lax.optimization_barrier((value, *earlier))[0]


def nt(left, right):
    return lax.dot_general(left, right, (((1,), (1,)), ((), ())), preferred_element_type=F32)


def chosen(ids):
    first, second = ids[0:1, :] == 0, ids[1:2, :] == 0
    count = ids.shape[1]
    named = jnp.where(first | second, 1.0, 0.0).astype(F32)
    at = lax.broadcasted_iota(jnp.int32, (count, count), 0)
    upto = lax.broadcasted_iota(jnp.int32, (count, count), 1)
    ones = jnp.where(at <= upto, 1.0, 0.0).astype(BF16)
    wide = jnp.broadcast_to(named, (16, count)).astype(BF16)
    rank = jnp.dot(wide, ones, preferred_element_type=F32)
    slot = lax.broadcasted_iota(jnp.int32, (CAP, count), 0).astype(F32) + 1.0
    return jnp.where((rank == slot) & (named > 0.0), 1.0, 0.0).astype(F32), first, second


PICK = 1536


def pick_kernel(ids_ref, tokens, grads, out_ref, tokens_v, grads_v, sems):
    copies = []
    for c in range(tokens.shape[1] // PICK):
        part = pl.ds(c * PICK, PICK)
        pair = (
            pltpu.make_async_copy(tokens.at[:, part], tokens_v.at[:, part], sems.at[0, c]),
            pltpu.make_async_copy(grads.at[:, part], grads_v.at[:, part], sems.at[1, c]),
        )
        for copy in pair:
            copy.start()
        copies.append(pair)
    onehot = chosen(ids_ref[...])[0].astype(BF16)
    for c, pair in enumerate(copies):
        part = slice(c * PICK, (c + 1) * PICK)
        for copy in pair:
            copy.wait()
        out_ref[:CAP, part] = jnp.dot(onehot, tokens_v[:, part], preferred_element_type=F32).astype(BF16)
        out_ref[CAP:, part] = jnp.dot(onehot, grads_v[:, part], preferred_element_type=F32).astype(BF16)


def pick(ids, tokens, grads):
    count, width = tokens.shape
    held = pl.BlockSpec(memory_space=pltpu.VMEM)
    anywhere = pl.BlockSpec(memory_space=pl.ANY)
    return pl.pallas_call(
        pick_kernel,
        out_shape=jax.ShapeDtypeStruct((2 * CAP, width), BF16),
        in_specs=[held, anywhere, anywhere],
        out_specs=held,
        scratch_shapes=[
            pltpu.VMEM((count, width), BF16),
            pltpu.VMEM((count, width), BF16),
            pltpu.SemaphoreType.DMA((2, width // PICK)),
        ],
        compiler_params=pltpu.CompilerParams(vmem_limit_bytes=60 * MIB),
        cost_estimate=pl.CostEstimate(flops=2 * 2 * 16 * 128 * width, bytes_accessed=4 * 128 * width, transcendentals=0),
        name="pick",
    )(ids, tokens, grads)


CHUNK = 1024
WIDE = 2 * CHUNK


def expert_kernel(rings, *refs):
    places = sum(len(ring) for ring in rings)
    count, made = 4 * places, 4 * len(rings)
    blocks, (up_a, up_b, down_a, down_b), outs = refs[:count], refs[count : count + 4], refs[count + 4 : count + 4 + made]
    rows_v, up_a_v, up_b_v, down_a_v, down_b_v, *held, row_sems, sems, out_sems = refs[count + 4 + made :]
    width, hidden = up_a.shape
    rows_in, copies = [], []
    for c in range(width // CHUNK):
        if c % 2 == 0:
            wide = pl.ds(c * CHUNK, WIDE)
            rows_in.append(
                [
                    pltpu.make_async_copy(block.at[:, wide], rows_v.at[i, :, wide], row_sems.at[i, c // 2])
                    for i, block in enumerate(blocks)
                ]
            )
            for copy in rows_in[-1]:
                copy.start()
        part = pl.ds(c * CHUNK, CHUNK)
        group = (
            pltpu.make_async_copy(up_a.at[part, :], up_a_v.at[part, :], sems.at[0, c]),
            pltpu.make_async_copy(up_b.at[part, :], up_b_v.at[part, :], sems.at[1, c]),
            pltpu.make_async_copy(down_a.at[:, part], down_a_v.at[:, part], sems.at[2, c]),
            pltpu.make_async_copy(down_b.at[:, part], down_b_v.at[:, part], sems.at[3, c]),
        )
        for copy in group:
            copy.start()
        copies.append(group)
    pre_a = pre_b = back_a = back_b = jnp.zeros((count * CAP, hidden), F32)
    for c in range(width // CHUNK):
        part = slice(c * CHUNK, (c + 1) * CHUNK)
        if c % 2 == 0:
            for copy in rows_in[c // 2]:
                copy.wait()
        for copy in copies[c]:
            copy.wait()
        ins = rows_v[:, :CAP, part].reshape(count * CAP, CHUNK)
        grads = rows_v[:, CAP:, part].reshape(count * CAP, CHUNK)
        pre_a += jnp.dot(ins, up_a_v[part, :], preferred_element_type=F32)
        pre_b += jnp.dot(ins, up_b_v[part, :], preferred_element_type=F32)
        back_a += nt(grads, down_a_v[:, part])
        back_b += nt(grads, down_b_v[:, part])

    def hidden_grad(pre, back):
        sig = 1.0 / (1.0 + jnp.exp(-pre))
        return (back * sig * (1.0 + pre * (1.0 - sig))).astype(BF16)

    grad_a, grad_b = hidden_grad(pre_a, back_a), hidden_grad(pre_b, back_b)
    leaving = []
    for c in range(width // CHUNK):
        part = slice(c * CHUNK, (c + 1) * CHUNK)
        sums = nt(grad_a, up_a_v[part, :]) + nt(grad_b, up_b_v[part, :])
        for ring, members in enumerate(rings):
            for x in range(4):
                at = 4 * ring + x
                for slot, z in enumerate(members):
                    rows = slice(slot * CAP, (slot + 1) * CAP)
                    held[at][rows, part] = sums[(4 * z + x) * CAP : (4 * z + x + 1) * CAP].astype(held[at].dtype)
                if c % 2 == 1:
                    wide = pl.ds((c - 1) * CHUNK, WIDE)
                    leaving.append(
                        pltpu.make_async_copy(held[at].at[:, wide], outs[at].at[:, wide], out_sems.at[at, c // 2])
                    )
                    leaving[-1].start()
    for copy in leaving:
        copy.wait()


def expert(blocks, weights, rings):
    width, hidden = weights[0].shape
    rows = len(blocks) * CAP
    anywhere = pl.BlockSpec(memory_space=pl.ANY)
    shapes = [(len(members) * CAP, width) for members in rings for _ in range(4)]
    kinds = [F32, BF16, F32, BF16] * len(rings)
    return pl.pallas_call(
        functools.partial(expert_kernel, rings),
        out_shape=tuple(jax.ShapeDtypeStruct(shape, kind) for shape, kind in zip(shapes, kinds)),
        in_specs=[anywhere] * (len(blocks) + 4),
        out_specs=(anywhere,) * len(shapes),
        scratch_shapes=[
            pltpu.VMEM((len(blocks), 2 * CAP, width), BF16),
            pltpu.VMEM((width, hidden), BF16),
            pltpu.VMEM((width, hidden), BF16),
            pltpu.VMEM((hidden, width), BF16),
            pltpu.VMEM((hidden, width), BF16),
            *(pltpu.VMEM(shape, kind) for shape, kind in zip(shapes, kinds)),
            pltpu.SemaphoreType.DMA((len(blocks), width // WIDE)),
            pltpu.SemaphoreType.DMA((4, width // CHUNK)),
            pltpu.SemaphoreType.DMA((len(shapes), width // WIDE)),
        ],
        compiler_params=pltpu.CompilerParams(vmem_limit_bytes=60 * MIB),
        cost_estimate=pl.CostEstimate(
            flops=2 * 3 * rows * width * 2 * hidden, bytes_accessed=16 * width * hidden, transcendentals=0
        ),
        name="expert",
    )(*blocks, *weights)


class Lane:
    def __init__(self, depth):
        self.depth, self.done, self.waits = depth, [], {}

    def hold(self, at, *earlier):
        self.waits[at] = (*self.waits.get(at, ()), *earlier)

    def send(self, value, move):
        waits = self.waits.pop(len(self.done), ())
        if len(self.done) >= self.depth:
            waits = (self.done[-self.depth], *waits)
        if waits:
            value = after(value, *waits)
        self.done.append(move(value))
        return self.done[-1]

    def ring(self, value, axis, step):
        return self.send(value, lambda v: mirrored(v, axis, step))

    def straight(self, value, axis, step):
        return self.send(value, lambda v: hop(v, axis, step))


def gather_ring(lane, block, axis):
    behind, ahead = lane.ring(block, axis, 1), lane.ring(block, axis, -1)
    return block, behind, ahead, lane.ring(behind, axis, 1)


def scatter_ring(lane, to_prev, to_next, far, axis):
    passing = lane.ring(far, axis, 1)
    from_ahead = lane.ring(to_prev, axis, -1)
    onward = (to_next + passing.astype(F32)).astype(BF16)
    return from_ahead, lane.ring(onward, axis, 1)


def arrived(stay, got):
    return stay + got[0].astype(F32) + got[1].astype(F32)


def place_kernel(ids_ref, share_ref, stay_ref, x_a, x_b, z_a, z_b, out_ref):
    onehot, first, second = chosen(ids_ref[...])
    share = share_ref[...]
    coef = jnp.where(first, share, jnp.where(second, 1.0 - share, 0.0))
    scale = jnp.sum(onehot * coef, axis=1, keepdims=True)
    spread = onehot.T.astype(BF16)
    total = stay_ref[...]
    for ref in (x_a, x_b, z_a, z_b):
        total += ref[...].astype(F32)
    result = (scale * total).astype(BF16)
    out_ref[...] = jnp.dot(spread, result, preferred_element_type=F32).astype(BF16)


def place(ids, share, stay, *got):
    count, width = ids.shape[1], stay.shape[1]
    part = width // 3
    return pl.pallas_call(
        place_kernel,
        grid=(3,),
        out_shape=jax.ShapeDtypeStruct((count, width), BF16),
        in_specs=[pl.BlockSpec(ids.shape, lambda i: (0, 0)), pl.BlockSpec(share.shape, lambda i: (0, 0))]
        + [pl.BlockSpec((CAP, part), lambda i: (0, i))] * (1 + len(got)),
        out_specs=pl.BlockSpec((count, part), lambda i: (0, i)),
        compiler_params=pltpu.CompilerParams(vmem_limit_bytes=24 * MIB),
        cost_estimate=pl.CostEstimate(flops=2 * 16 * 128 * width, bytes_accessed=2 * 128 * width, transcendentals=0),
        name="place",
    )(ids, share, stay, *got)


def swap(value, axis, partner):
    size = lax.axis_size(axis)
    pairs = [(2 * i + core, 2 * partner(core, i) + core) for i in range(size) for core in range(2)]
    return lax.ppermute(value, (axis, "core"), pairs)


def outer_sum(lane, term):
    def near(core, i):
        return i ^ 1 if core == 0 else (i + 1) % 4 if i % 2 else (i - 1) % 4

    term = term + lane.send(term, lambda v: swap(v, "y", near))
    term = term + lane.send(term, lambda v: swap(v, "y", lambda core, i: near(1 - core, i)))
    return term + lane.send(term, lambda v: swap(v, "zlo", lambda core, i: 1 - i))


def per_device(
    tokens, grad_out, expert_ids, gate_share, up_weight, down_weight, local_keys, outer_keys, momentum
):
    ids = expert_ids[0].T
    up, down = up_weight[0], down_weight[0]
    over_x, over_z, rest = Lane(2), Lane(1), Lane(1)
    up_other, down_other = hop(up, "core", 1), hop(down, "core", 1)
    mine = pick(ids, tokens[0], grad_out[0])
    own_x = gather_ring(over_x, mine, "x")
    _, behind, ahead, far = gather_ring(over_z, mine, "zh")

    columns, width = outer_keys.shape[1], momentum.shape[1]
    replicas = columns // width
    place_at = lax.axis_index("zlo") * lax.axis_size("y") + lax.axis_index("y")
    held = (lax.broadcasted_iota(jnp.int32, (1, columns), 1) // width) == place_at
    lead = 1.0 + OUTER_BETA
    term = jnp.where(held, OUTER_BETA**2 * jnp.tile(momentum, (1, replicas)), 0.0) - (lead / replicas) * local_keys[0]
    step = lead * outer_keys + outer_sum(rest, after(term, own_x[1]))
    new_outer = outer_keys - OUTER_RATE * step
    share = lax.dynamic_slice_in_dim(step, place_at * width, width, 1)
    new_momentum = OUTER_BETA * momentum + (share - OUTER_BETA**2 * momentum) / lead

    over_x.hold(3, up_other)
    over_x.hold(4, down_other)
    over_x.hold(7, rest.done[0])
    over_x.hold(9, rest.done[1])
    behind_x = gather_ring(over_x, behind, "x")
    ahead_x = gather_ring(over_x, ahead, "x")
    weights = (up, up_other, down, down_other)
    near = expert((*own_x, *behind_x, *ahead_x), weights, ((1, 2), (0,)))
    over_x.hold(11, near[0])
    over_x.hold(12, rest.done[2])
    far_x = gather_ring(over_x, far, "x")
    stay, prev, nxt, far = near[:4]
    pair = arrived(stay, scatter_ring(over_x, prev, nxt, far, "x"))
    over_x.depth = 3
    stay, prev, nxt, far = expert(far_x, weights, ((0,),))
    far = arrived(stay, scatter_ring(over_x, prev, nxt, far, "x"))
    back_z = Lane(2)
    from_ahead = back_z.ring(pair[:CAP].astype(BF16), "zh", -1)
    passing = back_z.ring(far.astype(BF16), "zh", 1)
    from_behind = back_z.ring((pair[CAP:] + passing.astype(F32)).astype(BF16), "zh", 1)
    stay, prev, nxt, far = near[4:]
    got_x = scatter_ring(over_x, prev, nxt, far, "x")
    input_grad = place(ids, gate_share, stay, *got_x, from_ahead, from_behind)
    return input_grad[None], new_outer, new_momentum, new_outer.astype(BF16)


def solution(mesh):
    fine = Mesh(mesh.devices.reshape(2, 4, 4, 4, 2), ("zlo", "y", "x", "zh", "core"))
    replica, fsdp = ("zlo", "y"), ("x", "zh", "core")
    return jax.shard_map(
        per_device,
        mesh=fine,
        in_specs=(
            P(replica, fsdp, None),
            P(replica, fsdp, None),
            P(replica, fsdp, None),
            P(replica, fsdp),
            P(replica, None, fsdp),
            P(replica, fsdp, None),
            P(replica, fsdp, None),
            P(fsdp, None),
            P(fsdp, replica),
        ),
        out_specs=(P(replica, fsdp, None), P(fsdp, None), P(fsdp, replica), P(fsdp, None)),
        check_vma=False,
    )
```

profile of v0, /device:TPU:6, one launch (start us, length us, event | category | flops | bytes accessed | tf_op | source)
XLA Modules:
  0.0 139.3 jit_solution(2406242627879450642)
XLA Ops:
  1.2 3.5 %pick.1.refs_0_ = bf16[32,6144]{1,0:T(8,128)(2,1)} custom-call(s32[2,128]{1,0:T(2,128)} %bitcast.14, bf16[128,6144]{1,0:T(8,128)(2,1)} %bitcast.22, bf16[128,6144]{1,0:T(8,128)(2,1)} %bitcast.23), custom_call_target="tpu_custom_call" | custom-call | flops 50331648 | bytes 3145728 | tf_op jit(solution)/shard_map/pick/pallas_call | solution.py:80
  4.8 2.3 %collective-permute-start = (bf16[32,6144]{1,0:T(8,128)(2,1)}, bf16[32,6144]{1,0:T(8,128)(2,1)}, u32[]{:S(2)}, u32[]{:S(2)}) collective-permute-start(bf16[32,6144]{1,0:T(8,128)(2,1)} %pick.1.refs_0_), channel_id=1, source_target_pairs={{0,8},{1,25},{8,16},{9,1},{16,24},{17,9},{24,0},{25,17},{2,10},{3,... | collective-permute-start | bytes 1179656 | tf_op jit(solution)/shard_map/ppermute | solution.py:29
  10.2 2.8 %collective-permute-done.refs_1_ = bf16[32,6144]{1,0:T(8,128)(2,1)} collective-permute-done((bf16[32,6144]{1,0:T(8,128)(2,1)}, bf16[32,6144]{1,0:T(8,128)(2,1)}, u32[]{:S(2)}, u32[]{:S(2)}) %collective-permute-start) | collective-permute-done | bytes 393248 | tf_op jit(solution)/shard_map/ppermute | solution.py:29
  13.0 3.4 %collective-permute-start.2 = (bf16[32,6144]{1,0:T(8,128)(2,1)}, bf16[32,6144]{1,0:T(8,128)(2,1)}, u32[]{:S(2)}, u32[]{:S(2)}) collective-permute-start(bf16[32,6144]{1,0:T(8,128)(2,1)} %collective-permute-done.refs_1_), channel_id=1, source_target_pairs={{0,8},{1,25},{8,16},{9,1},{16,24},{17,9},{24,0},{25,17},{2,10},{3,... | collective-permute-start | bytes 1179656 | tf_op jit(solution)/shard_map/ppermute | solution.py:29
  16.4 2.9 %collective-permute-done.3.refs_4_ = bf16[32,6144]{1,0:T(8,128)(2,1)} collective-permute-done((bf16[32,6144]{1,0:T(8,128)(2,1)}, bf16[32,6144]{1,0:T(8,128)(2,1)}, u32[]{:S(2)}, u32[]{:S(2)}) %collective-permute-start.3) | collective-permute-done | bytes 393248 | tf_op jit(solution)/shard_map/ppermute | solution.py:29
  22.6 5.6 %collective-permute-start.9 = (bf16[32,6144]{1,0:T(8,128)(2,1)}, bf16[32,6144]{1,0:T(8,128)(2,1)S(1)}, u32[]{:S(2)}, u32[]{:S(2)}) collective-permute-start(bf16[32,6144]{1,0:T(8,128)(2,1)} %pick.1.refs_0_), channel_id=1, source_target_pairs={{0,6},{1,3},{2,0},{3,5},{4,2},{5,7},{6,4},{7,1},{8,14},{9,11},{10,... | collective-permute-start | bytes 1179656 | tf_op jit(solution)/shard_map/ppermute | solution.py:29
  32.8 2.4 %collective-permute-start.8 = (bf16[32,6144]{1,0:T(8,128)(2,1)}, bf16[32,6144]{1,0:T(8,128)(2,1)S(1)}, u32[]{:S(2)}, u32[]{:S(2)}) collective-permute-start(bf16[32,6144]{1,0:T(8,128)(2,1)} %collective-permute-done.5.refs_5_), channel_id=1, source_target_pairs={{0,8},{1,25},{8,16},{9,1},{16,24},{17,9},{24,0},{25,17},{2,10},{3,... | collective-permute-start | bytes 1179656 | tf_op jit(solution)/shard_map/ppermute | solution.py:29
  35.1 3.1 %collective-permute-done.9.refs_8_ = bf16[32,6144]{1,0:T(8,128)(2,1)S(1)} collective-permute-done((bf16[32,6144]{1,0:T(8,128)(2,1)}, bf16[32,6144]{1,0:T(8,128)(2,1)S(1)}, u32[]{:S(2)}, u32[]{:S(2)}) %collective-permute-start.9) | collective-permute-done | bytes 393248 | tf_op jit(solution)/shard_map/ppermute | solution.py:29
  40.4 3.3 %collective-permute-start.15 = (f32[192,512]{0,1:T(8,128)S(1)}, f32[192,512]{0,1:T(8,128)S(1)}, u32[]{:S(2)}, u32[]{:S(2)}) collective-permute-start(f32[192,512]{0,1:T(8,128)S(1)} %add.52), channel_id=1, source_target_pairs={{0,96},{1,33},{32,64},{33,1},{64,32},{65,97},{96,0},{97,65},{2,98}... | collective-permute-start | bytes 1179656 | tf_op jit(solution)/shard_map/ppermute | solution.py:269
  43.7 2.9 %collective-permute-start.14 = (bf16[32,6144]{1,0:T(8,128)(2,1)}, bf16[32,6144]{1,0:T(8,128)(2,1)S(1)}, u32[]{:S(2)}, u32[]{:S(2)}) collective-permute-start(bf16[32,6144]{1,0:T(8,128)(2,1)} %collective-permute-done.3.refs_4_), channel_id=1, source_target_pairs={{0,2},{1,7},{2,4},{3,1},{4,6},{5,3},{6,0},{7,5},{8,10},{9,15},{10,... | collective-permute-start | bytes 1179656 | tf_op jit(solution)/shard_map/ppermute | solution.py:29
  47.8 2.8 %collective-permute-start.13 = (bf16[32,6144]{1,0:T(8,128)(2,1)S(1)}, bf16[32,6144]{1,0:T(8,128)(2,1)S(1)}, u32[]{:S(2)}, u32[]{:S(2)}) collective-permute-start(bf16[32,6144]{1,0:T(8,128)(2,1)S(1)} %collective-permute-done.10.refs_9_), channel_id=1, source_target_pairs={{0,8},{1,25},{8,16},{9,1},{16,24},{17,9},{24,0},{25,17},{2,10},{3,... | collective-permute-start | bytes 1179656 | tf_op jit(solution)/shard_map/ppermute | solution.py:29
  50.9 4.3 %collective-permute-done.14.refs_0_ = bf16[32,6144]{1,0:T(8,128)(2,1)S(1)} collective-permute-done((bf16[32,6144]{1,0:T(8,128)(2,1)}, bf16[32,6144]{1,0:T(8,128)(2,1)S(1)}, u32[]{:S(2)}, u32[]{:S(2)}) %collective-permute-start.14) | collective-permute-done | bytes 393248 | tf_op jit(solution)/shard_map/ppermute | solution.py:29
  55.2 4.7 %collective-permute-done.12.refs_10_ = bf16[32,6144]{1,0:T(8,128)(2,1)S(1)} collective-permute-done((bf16[32,6144]{1,0:T(8,128)(2,1)S(1)}, bf16[32,6144]{1,0:T(8,128)(2,1)S(1)}, u32[]{:S(2)}, u32[]{:S(2)}) %collective-permute-start.12) | collective-permute-done | bytes 393248 | tf_op jit(solution)/shard_map/ppermute | solution.py:29
  64.3 11.0 %expert.2 = (f32[32,6144]{1,0:T(8,128)}, bf16[32,6144]{1,0:T(8,128)(2,1)}, f32[32,6144]{1,0:T(8,128)}, bf16[32,6144]{1,0:T(8,128)(2,1)}, f32[16,6144]{1,0:T(8,12...) custom-call(bf16[32,6144]{1,0:T(8,128)(2,1)} %pick.1.refs_0_, ...), custom_call_target="tpu_custom_call" | custom-call | flops 3623878656 | bytes 25165824 | tf_op jit(solution)/shard_map/expert/pallas_call | solution.py:174
  75.3 2.4 %collective-permute-start.18 = (bf16[32,6144]{1,0:T(8,128)(2,1)}, bf16[32,6144]{1,0:T(8,128)(2,1)S(1)}, u32[]{:S(2)}, u32[]{:S(2)}) collective-permute-start(bf16[32,6144]{1,0:T(8,128)(2,1)} %collective-permute-done.16.refs_1_), channel_id=1, source_target_pairs={{0,8},{1,25},{8,16},{9,1},{16,24},{17,9},{24,0},{25,17},{2,10},{3,... | collective-permute-start | bytes 1179656 | tf_op jit(solution)/shard_map/ppermute | solution.py:29
  84.1 9.9 %expert.3 = (f32[16,6144]{1,0:T(8,128)}, bf16[16,6144]{1,0:T(8,128)(2,1)}, f32[16,6144]{1,0:T(8,128)}, bf16[16,6144]{1,0:T(8,128)(2,1)}) custom-call(bf16[32,6144]{1,0:T(8,128)(2,1)} %copy-done.7, bf16[32,6144]{1,0:T(8,128)(2,1)} %collective-permute-done.16.refs_1_, bf16[32,6144]{1,0:T(8,128)(2,1)} %collective-permute-done.17.refs_2_, ...), custom_call_target="tpu_custom_call" | custom-call | flops 1207959552 | bytes 25165824 | tf_op jit(solution)/shard_map/expert/pallas_call | solution.py:174
  94.0 3.8 %collective-permute-start.24 = (bf16[16,6144]{1,0:T(8,128)(2,1)}, bf16[16,6144]{1,0:T(8,128)(2,1)S(1)}, u32[]{:S(2)}, u32[]{:S(2)}) collective-permute-start(bf16[16,6144]{1,0:T(8,128)(2,1)} %get-tuple-element.69), channel_id=1, source_target_pairs={{0,8},{1,25},{8,16},{9,1},{16,24},{17,9},{24,0},{25,17},{2,10},{3,... | collective-permute-start | bytes 589832 | tf_op jit(solution)/shard_map/ppermute | solution.py:29
  101.8 3.6 %collective-permute-start.25 = (bf16[16,6144]{1,0:T(8,128)(2,1)S(1)}, bf16[16,6144]{1,0:T(8,128)(2,1)S(1)}, u32[]{:S(2)}, u32[]{:S(2)}) collective-permute-start(bf16[16,6144]{1,0:T(8,128)(2,1)S(1)} %copy-done.22), channel_id=1, source_target_pairs={{0,8},{1,25},{8,16},{9,1},{16,24},{17,9},{24,0},{25,17},{2,10},{3,... | collective-permute-start | bytes 589832 | tf_op jit(solution)/shard_map/ppermute | solution.py:29
  107.6 3.7 %collective-permute-start.27 = (bf16[16,6144]{1,0:T(8,128)(2,1)S(1)}, bf16[16,6144]{1,0:T(8,128)(2,1)S(1)}, u32[]{:S(2)}, u32[]{:S(2)}) collective-permute-start(bf16[16,6144]{1,0:T(8,128)(2,1)S(1)} %add_convert_fusion.2), channel_id=1, source_target_pairs={{0,8},{1,25},{8,16},{9,1},{16,24},{17,9},{24,0},{25,17},{2,10},{3,... | collective-permute-start | bytes 589832 | tf_op jit(solution)/shard_map/ppermute | solution.py:29
  112.6 3.7 %collective-permute-done.27 = bf16[16,6144]{1,0:T(8,128)(2,1)S(1)} collective-permute-done((bf16[16,6144]{1,0:T(8,128)(2,1)S(1)}, bf16[16,6144]{1,0:T(8,128)(2,1)S(1)}, u32[]{:S(2)}, u32[]{:S(2)}) %collective-permute-start.27) | collective-permute-done | bytes 196640 | tf_op jit(solution)/shard_map/ppermute | solution.py:29
  116.3 2.0 %collective-permute-done.20 = bf16[16,6144]{1,0:T(8,128)(2,1)S(1)} collective-permute-done((bf16[16,6144]{1,0:T(8,128)(2,1)}, bf16[16,6144]{1,0:T(8,128)(2,1)S(1)}, u32[]{:S(2)}, u32[]{:S(2)}) %collective-permute-start.20) | collective-permute-done | bytes 196640 | tf_op jit(solution)/shard_map/ppermute | solution.py:29
  122.5 4.1 %collective-permute-done.30 = bf16[16,6144]{1,0:T(8,128)(2,1)S(1)} collective-permute-done((bf16[16,6144]{1,0:T(8,128)(2,1)S(1)}, bf16[16,6144]{1,0:T(8,128)(2,1)S(1)}, u32[]{:S(2)}, u32[]{:S(2)}) %collective-permute-start.30) | collective-permute-done | bytes 196640 | tf_op jit(solution)/shard_map/ppermute | solution.py:29
  128.7 7.9 %collective-permute-done.31.z_b = bf16[16,6144]{1,0:T(8,128)(2,1)S(1)} collective-permute-done((bf16[16,6144]{1,0:T(8,128)(2,1)S(1)}, bf16[16,6144]{1,0:T(8,128)(2,1)S(1)}, u32[]{:S(2)}, u32[]{:S(2)}) %collective-permute-start.31) | collective-permute-done | bytes 196640 | tf_op jit(solution)/shard_map/ppermute | solution.py:29
  136.6 2.7 %place.1 = bf16[128,6144]{1,0:T(8,128)(2,1)} custom-call(s32[2,128]{1,0:T(2,128)S(1)} %bitcast.15, f32[1,128]{1,0:T(1,128)S(1)} %copy-done.2, f32[16,6144]{1,0:T(8,128)S(1)} %copy-done, bf16[16,6144]{1,0:T(8,128)(2,1)S(1)} %collective-permute-done.21.x_a, bf16[16,6144]{1,0:T(8,128)(2,1)S(1)} %collective-permute-done.28.x_b, ...), custom_call_target="tpu_custom_call" | custom-call | flops 25165824 | bytes 1572864 | tf_op jit(solution)/shard_map/place/pallas_call | solution.py:253
  (108 shorter events, 39.6 us)
Async XLA Ops:
  0.6 18.7 %collective-permute-start.4 = (bf16[6144,256]{1,0:T(8,128)(2,1)}, bf16[6144,256]{1,0:T(8,128)(2,1)S(1)}, u32[]{:S(2)}, u32[]{:S(2)}) collective-permute-start(bf16[6144,256]{1,0:T(8,128)(2,1)} %bitcast.16), channel_id=1, source_target_pairs={{0,1},{1,0},{2,3},{3,2},{4,5},{5,4},{6,7},{7,6},{8,9},{9,8},{10,11... | collective-permute-start | bytes 9437192 | tf_op jit(solution)/shard_map/ppermute | solution.py:20
  0.7 27.4 %collective-permute-start.6 = (bf16[256,6144]{1,0:T(8,128)(2,1)}, bf16[256,6144]{1,0:T(8,128)(2,1)}, u32[]{:S(2)}, u32[]{:S(2)}) collective-permute-start(bf16[256,6144]{1,0:T(8,128)(2,1)} %bitcast.19), channel_id=1, source_target_pairs={{0,1},{1,0},{2,3},{3,2},{4,5},{5,4},{6,7},{7,6},{8,9},{9,8},{10,11... | collective-permute-start | bytes 9437192 | tf_op jit(solution)/shard_map/ppermute | solution.py:20
  7.1 12.2 %collective-permute-start.3 = (bf16[32,6144]{1,0:T(8,128)(2,1)}, bf16[32,6144]{1,0:T(8,128)(2,1)}, u32[]{:S(2)}, u32[]{:S(2)}) collective-permute-start(bf16[32,6144]{1,0:T(8,128)(2,1)} %pick.1.refs_0_), channel_id=1, source_target_pairs={{0,2},{1,7},{2,4},{3,1},{4,6},{5,3},{6,0},{7,5},{8,10},{9,15},{10,... | collective-permute-start | bytes 1179656 | tf_op jit(solution)/shard_map/ppermute | solution.py:29
  8.6 10.7 %collective-permute-start.1 = (bf16[32,6144]{1,0:T(8,128)(2,1)}, bf16[32,6144]{1,0:T(8,128)(2,1)S(1)}, u32[]{:S(2)}, u32[]{:S(2)}) collective-permute-start(bf16[32,6144]{1,0:T(8,128)(2,1)} %pick.1.refs_0_), channel_id=1, source_target_pairs={{0,24},{1,9},{8,0},{9,17},{16,8},{17,25},{24,16},{25,1},{2,26},{3,... | collective-permute-start | bytes 1179656 | tf_op jit(solution)/shard_map/ppermute | solution.py:29
  13.0 15.2 %collective-permute-start.2 = (bf16[32,6144]{1,0:T(8,128)(2,1)}, bf16[32,6144]{1,0:T(8,128)(2,1)}, u32[]{:S(2)}, u32[]{:S(2)}) collective-permute-start(bf16[32,6144]{1,0:T(8,128)(2,1)} %collective-permute-done.refs_1_), channel_id=1, source_target_pairs={{0,8},{1,25},{8,16},{9,1},{16,24},{17,9},{24,0},{25,17},{2,10},{3,... | collective-permute-start | bytes 1179656 | tf_op jit(solution)/shard_map/ppermute | solution.py:29
  20.1 12.7 %collective-permute-start.5 = (bf16[32,6144]{1,0:T(8,128)(2,1)}, bf16[32,6144]{1,0:T(8,128)(2,1)}, u32[]{:S(2)}, u32[]{:S(2)}) collective-permute-start(bf16[32,6144]{1,0:T(8,128)(2,1)} %collective-permute-done.3.refs_4_), channel_id=1, source_target_pairs={{0,8},{1,25},{8,16},{9,1},{16,24},{17,9},{24,0},{25,17},{2,10},{3,... | collective-permute-start | bytes 1179656 | tf_op jit(solution)/shard_map/ppermute | solution.py:29
  22.6 15.6 %collective-permute-start.9 = (bf16[32,6144]{1,0:T(8,128)(2,1)}, bf16[32,6144]{1,0:T(8,128)(2,1)S(1)}, u32[]{:S(2)}, u32[]{:S(2)}) collective-permute-start(bf16[32,6144]{1,0:T(8,128)(2,1)} %pick.1.refs_0_), channel_id=1, source_target_pairs={{0,6},{1,3},{2,0},{3,5},{4,2},{5,7},{6,4},{7,1},{8,14},{9,11},{10,... | collective-permute-start | bytes 1179656 | tf_op jit(solution)/shard_map/ppermute | solution.py:29
  28.2 10.4 %collective-permute-start.7 = (bf16[32,6144]{1,0:T(8,128)(2,1)}, bf16[32,6144]{1,0:T(8,128)(2,1)S(1)}, u32[]{:S(2)}, u32[]{:S(2)}) collective-permute-start(bf16[32,6144]{1,0:T(8,128)(2,1)} %collective-permute-done.3.refs_4_), channel_id=1, source_target_pairs={{0,24},{1,9},{8,0},{9,17},{16,8},{17,25},{24,16},{25,1},{2,26},{3,... | collective-permute-start | bytes 1179656 | tf_op jit(solution)/shard_map/ppermute | solution.py:29
  31.1 9.3 %collective-permute-start.11 = (f32[192,512]{0,1:T(8,128)S(1)}, f32[192,512]{0,1:T(8,128)S(1)}, u32[]{:S(2)}, u32[]{:S(2)}) collective-permute-start(f32[192,512]{0,1:T(8,128)S(1)} %bitcast_subtract_fusion), channel_id=1, source_target_pairs={{0,32},{1,97},{32,0},{33,65},{64,96},{65,33},{96,64},{97,1},{2,34}... | collective-permute-start | bytes 1179656 | tf_op jit(solution)/shard_map/ppermute | solution.py:269
  32.8 13.8 %collective-permute-start.8 = (bf16[32,6144]{1,0:T(8,128)(2,1)}, bf16[32,6144]{1,0:T(8,128)(2,1)S(1)}, u32[]{:S(2)}, u32[]{:S(2)}) collective-permute-start(bf16[32,6144]{1,0:T(8,128)(2,1)} %collective-permute-done.5.refs_5_), channel_id=1, source_target_pairs={{0,8},{1,25},{8,16},{9,1},{16,24},{17,9},{24,0},{25,17},{2,10},{3,... | collective-permute-start | bytes 1179656 | tf_op jit(solution)/shard_map/ppermute | solution.py:29
  38.6 9.2 %collective-permute-start.10 = (bf16[32,6144]{1,0:T(8,128)(2,1)S(1)}, bf16[32,6144]{1,0:T(8,128)(2,1)S(1)}, u32[]{:S(2)}, u32[]{:S(2)}) collective-permute-start(bf16[32,6144]{1,0:T(8,128)(2,1)S(1)} %collective-permute-done.9.refs_8_), channel_id=1, source_target_pairs={{0,8},{1,25},{8,16},{9,1},{16,24},{17,9},{24,0},{25,17},{2,10},{3,... | collective-permute-start | bytes 1179656 | tf_op jit(solution)/shard_map/ppermute | solution.py:29
  40.4 10.5 %collective-permute-start.15 = (f32[192,512]{0,1:T(8,128)S(1)}, f32[192,512]{0,1:T(8,128)S(1)}, u32[]{:S(2)}, u32[]{:S(2)}) collective-permute-start(f32[192,512]{0,1:T(8,128)S(1)} %add.52), channel_id=1, source_target_pairs={{0,96},{1,33},{32,64},{33,1},{64,32},{65,97},{96,0},{97,65},{2,98}... | collective-permute-start | bytes 1179656 | tf_op jit(solution)/shard_map/ppermute | solution.py:269
  43.7 11.5 %collective-permute-start.14 = (bf16[32,6144]{1,0:T(8,128)(2,1)}, bf16[32,6144]{1,0:T(8,128)(2,1)S(1)}, u32[]{:S(2)}, u32[]{:S(2)}) collective-permute-start(bf16[32,6144]{1,0:T(8,128)(2,1)} %collective-permute-done.3.refs_4_), channel_id=1, source_target_pairs={{0,2},{1,7},{2,4},{3,1},{4,6},{5,3},{6,0},{7,5},{8,10},{9,15},{10,... | collective-permute-start | bytes 1179656 | tf_op jit(solution)/shard_map/ppermute | solution.py:29
  46.6 13.3 %collective-permute-start.12 = (bf16[32,6144]{1,0:T(8,128)(2,1)S(1)}, bf16[32,6144]{1,0:T(8,128)(2,1)S(1)}, u32[]{:S(2)}, u32[]{:S(2)}) collective-permute-start(bf16[32,6144]{1,0:T(8,128)(2,1)S(1)} %collective-permute-done.9.refs_8_), channel_id=1, source_target_pairs={{0,24},{1,9},{8,0},{9,17},{16,8},{17,25},{24,16},{25,1},{2,26},{3,... | collective-permute-start | bytes 1179656 | tf_op jit(solution)/shard_map/ppermute | solution.py:29
  47.8 14.8 %collective-permute-start.13 = (bf16[32,6144]{1,0:T(8,128)(2,1)S(1)}, bf16[32,6144]{1,0:T(8,128)(2,1)S(1)}, u32[]{:S(2)}, u32[]{:S(2)}) collective-permute-start(bf16[32,6144]{1,0:T(8,128)(2,1)S(1)} %collective-permute-done.10.refs_9_), channel_id=1, source_target_pairs={{0,8},{1,25},{8,16},{9,1},{16,24},{17,9},{24,0},{25,17},{2,10},{3,... | collective-permute-start | bytes 1179656 | tf_op jit(solution)/shard_map/ppermute | solution.py:29
  59.9 15.4 %collective-permute-start.16 = (bf16[32,6144]{1,0:T(8,128)(2,1)S(1)}, bf16[32,6144]{1,0:T(8,128)(2,1)}, u32[]{:S(2)}, u32[]{:S(2)}) collective-permute-start(bf16[32,6144]{1,0:T(8,128)(2,1)S(1)} %collective-permute-done.14.refs_0_), channel_id=1, source_target_pairs={{0,8},{1,25},{8,16},{9,1},{16,24},{17,9},{24,0},{25,17},{2,10},{3,... | collective-permute-start | bytes 1179656 | tf_op jit(solution)/shard_map/ppermute | solution.py:29
  60.8 18.1 %collective-permute-start.22 = (f32[192,512]{0,1:T(8,128)}, f32[192,512]{0,1:T(8,128)}, u32[]{:S(2)}, u32[]{:S(2)}) collective-permute-start(f32[192,512]{0,1:T(8,128)} %add.53), channel_id=1, source_target_pairs={{0,128},{1,129},{128,0},{129,1},{2,130},{3,131},{130,2},{131,3},{4... | collective-permute-start | bytes 1179656 | tf_op jit(solution)/shard_map/ppermute | solution.py:269
  63.4 15.5 %collective-permute-start.17 = (bf16[32,6144]{1,0:T(8,128)(2,1)S(1)}, bf16[32,6144]{1,0:T(8,128)(2,1)}, u32[]{:S(2)}, u32[]{:S(2)}) collective-permute-start(bf16[32,6144]{1,0:T(8,128)(2,1)S(1)} %collective-permute-done.14.refs_0_), channel_id=1, source_target_pairs={{0,24},{1,9},{8,0},{9,17},{16,8},{17,25},{24,16},{25,1},{2,26},{3,... | collective-permute-start | bytes 1179656 | tf_op jit(solution)/shard_map/ppermute | solution.py:29
  78.9 15.1 %collective-permute-start.23 = (bf16[32,6144]{1,0:T(8,128)(2,1)}, bf16[32,6144]{1,0:T(8,128)(2,1)S(1)}, u32[]{:S(2)}, u32[]{:S(2)}) collective-permute-start(bf16[32,6144]{1,0:T(8,128)(2,1)} %get-tuple-element.68), channel_id=1, source_target_pairs={{0,8},{1,25},{8,16},{9,1},{16,24},{17,9},{24,0},{25,17},{2,10},{3,... | collective-permute-start | bytes 1179656 | tf_op jit(solution)/shard_map/ppermute | solution.py:29
  98.0 9.6 %collective-permute-start.26 = (bf16[32,6144]{1,0:T(8,128)(2,1)S(1)}, bf16[32,6144]{1,0:T(8,128)(2,1)S(1)}, u32[]{:S(2)}, u32[]{:S(2)}) collective-permute-start(bf16[32,6144]{1,0:T(8,128)(2,1)S(1)} %add_convert_fusion), channel_id=1, source_target_pairs={{0,8},{1,25},{8,16},{9,1},{16,24},{17,9},{24,0},{25,17},{2,10},{3,... | collective-permute-start | bytes 1179656 | tf_op jit(solution)/shard_map/ppermute | solution.py:29
  98.1 13.2 %collective-permute-start.19 = (bf16[32,6144]{1,0:T(8,128)(2,1)S(1)}, bf16[32,6144]{1,0:T(8,128)(2,1)S(1)}, u32[]{:S(2)}, u32[]{:S(2)}) collective-permute-start(bf16[32,6144]{1,0:T(8,128)(2,1)S(1)} %copy-done.20), channel_id=1, source_target_pairs={{0,24},{1,9},{8,0},{9,17},{16,8},{17,25},{24,16},{25,1},{2,26},{3,... | collective-permute-start | bytes 1179656 | tf_op jit(solution)/shard_map/ppermute | solution.py:29
  101.8 18.5 %collective-permute-start.25 = (bf16[16,6144]{1,0:T(8,128)(2,1)S(1)}, bf16[16,6144]{1,0:T(8,128)(2,1)S(1)}, u32[]{:S(2)}, u32[]{:S(2)}) collective-permute-start(bf16[16,6144]{1,0:T(8,128)(2,1)S(1)} %copy-done.22), channel_id=1, source_target_pairs={{0,8},{1,25},{8,16},{9,1},{16,24},{17,9},{24,0},{25,17},{2,10},{3,... | collective-permute-start | bytes 589832 | tf_op jit(solution)/shard_map/ppermute | solution.py:29
  111.5 15.1 %collective-permute-start.29 = (bf16[16,6144]{1,0:T(8,128)(2,1)S(1)}, bf16[16,6144]{1,0:T(8,128)(2,1)S(1)}, u32[]{:S(2)}, u32[]{:S(2)}) collective-permute-start(bf16[16,6144]{1,0:T(8,128)(2,1)S(1)} %slice.15), channel_id=1, source_target_pairs={{0,6},{1,3},{2,0},{3,5},{4,2},{5,7},{6,4},{7,1},{8,14},{9,11},{10,... | collective-permute-start | bytes 589832 | tf_op jit(solution)/shard_map/ppermute | solution.py:29
  126.6 10.0 %collective-permute-start.31 = (bf16[16,6144]{1,0:T(8,128)(2,1)S(1)}, bf16[16,6144]{1,0:T(8,128)(2,1)S(1)}, u32[]{:S(2)}, u32[]{:S(2)}) collective-permute-start(bf16[16,6144]{1,0:T(8,128)(2,1)S(1)} %fusion), channel_id=1, source_target_pairs={{0,2},{1,7},{2,4},{3,1},{4,6},{5,3},{6,0},{7,5},{8,10},{9,15},{10,... | collective-permute-start | bytes 589832 | tf_op jit(solution)/shard_map/ppermute | solution.py:29
  (31 other events, 507.3 us)
where the time goes:
time: 140 us; the launch traced here: 139 us
  starting transfers between devices  57.1 us (41%)
  waiting for transfers between devices  42.3 us (30%)
  Pallas kernels  27.1 us (19%)
  other arithmetic  7.19 us (5%)
  local copies, waits for them, and re-layouts  4.72 us (3%)
    ppermute x27, starting transfers between devices, mirrored(): return lax.ppermute(value, (axis, 'core'), pairs)  49.8 us
    ppermute x27, waiting for transfers between devices, mirrored(): return lax.ppermute(value, (axis, 'core'), pairs)  41.7 us
    pallas_call x2, Pallas kernels, expert(): pl.pallas_call(functools.partial(expert_kernel, rings), out_shape=tuple((...  20.8 us
    ppermute x3, starting transfers between devices, swap(): return lax.ppermute(value, (axis, 'core'), pairs)  6.69 us
    unnamed x49, local copies, waits for them, and re-layouts  4.7 us
    pallas_call x1, Pallas kernels, pick(): pl.pallas_call(pick_kernel, out_shape=jax.ShapeDtypeStruct((2 * CAP, widt...  3.54 us
  transfers between devices with their start and end apart: 32, of which 16 were waited for; matrix products, arithmetic and copies ran while one was open for 7% of the time, Pallas kernels for 18%

commit v1 on v0

--- a/solution.py
+++ b/solution.py
@@ -165,12 +165,12 @@
         copy.wait()
 
 
-def expert(blocks, weights, rings):
+def expert(blocks, weights, rings, added):
     width, hidden = weights[0].shape
     rows = len(blocks) * CAP
     anywhere = pl.BlockSpec(memory_space=pl.ANY)
     shapes = [(len(members) * CAP, width) for members in rings for _ in range(4)]
-    kinds = [F32, BF16, F32, BF16] * len(rings)
+    kinds = [kind for third in added for kind in (F32, BF16, third, BF16)]
     return pl.pallas_call(
         functools.partial(expert_kernel, rings),
         out_shape=tuple(jax.ShapeDtypeStruct(shape, kind) for shape, kind in zip(shapes, kinds)),
@@ -195,6 +195,10 @@
     )(*blocks, *weights)
 
 
+def after_all(values, *earlier):
+    return lax.optimization_barrier((*values, *earlier))[: len(values)]
+
+
 class Lane:
     def __init__(self, depth):
         self.depth, self.done, self.waits = depth, [], {}
@@ -223,25 +227,19 @@
     return block, behind, ahead, lane.ring(behind, axis, 1)
 
 
-def scatter_ring(lane, to_prev, to_next, far, axis):
-    passing = lane.ring(far, axis, 1)
-    from_ahead = lane.ring(to_prev, axis, -1)
-    onward = (to_next + passing.astype(F32)).astype(BF16)
-    return from_ahead, lane.ring(onward, axis, 1)
-
-
-def arrived(stay, got):
-    return stay + got[0].astype(F32) + got[1].astype(F32)
-
-
-def place_kernel(ids_ref, share_ref, stay_ref, x_a, x_b, z_a, z_b, out_ref):
+def joined(mine, passing):
+    return (mine + passing.astype(F32)).astype(BF16)
+
+
+def place_kernel(ids_ref, share_ref, stay_ref, *refs):
+    *got, out_ref = refs
     onehot, first, second = chosen(ids_ref[...])
     share = share_ref[...]
     coef = jnp.where(first, share, jnp.where(second, 1.0 - share, 0.0))
     scale = jnp.sum(onehot * coef, axis=1, keepdims=True)
     spread = onehot.T.astype(BF16)
     total = stay_ref[...]
-    for ref in (x_a, x_b, z_a, z_b):
+    for ref in got:
         total += ref[...].astype(F32)
     result = (scale * total).astype(BF16)
     out_ref[...] = jnp.dot(spread, result, preferred_element_type=F32).astype(BF16)
@@ -287,7 +285,9 @@
     up_other, down_other = hop(up, "core", 1), hop(down, "core", 1)
     mine = pick(ids, tokens[0], grad_out[0])
     own_x = gather_ring(over_x, mine, "x")
-    _, behind, ahead, far = gather_ring(over_z, mine, "zh")
+    behind = over_z.ring(mine, "zh", 1)
+    far = over_z.ring(behind, "zh", 1)
+    ahead = over_z.ring(mine, "zh", -1)
 
     columns, width = outer_keys.shape[1], momentum.shape[1]
     replicas = columns // width
@@ -295,34 +295,36 @@
     held = (lax.broadcasted_iota(jnp.int32, (1, columns), 1) // width) == place_at
     lead = 1.0 + OUTER_BETA
     term = jnp.where(held, OUTER_BETA**2 * jnp.tile(momentum, (1, replicas)), 0.0) - (lead / replicas) * local_keys[0]
-    step = lead * outer_keys + outer_sum(rest, after(term, own_x[1]))
-    new_outer = outer_keys - OUTER_RATE * step
-    share = lax.dynamic_slice_in_dim(step, place_at * width, width, 1)
-    new_momentum = OUTER_BETA * momentum + (share - OUTER_BETA**2 * momentum) / lead
-
+    summed = outer_sum(rest, after(term, own_x[1]))
     over_x.hold(3, up_other)
     over_x.hold(4, down_other)
     over_x.hold(7, rest.done[0])
     over_x.hold(9, rest.done[1])
     behind_x = gather_ring(over_x, behind, "x")
+    far_x = gather_ring(over_x, far, "x")
+    weights = (up, up_other, down, down_other)
+    near = expert((*own_x, *behind_x, *far_x), weights, ((1, 2), (0,)), (BF16, F32))
+    over_x.hold(11, near[0])
+    step = lead * outer_keys + after(summed, near[0])
+    new_outer = outer_keys - OUTER_RATE * step
+    share = lax.dynamic_slice_in_dim(step, place_at * width, width, 1)
+    new_momentum = OUTER_BETA * momentum + (share - OUTER_BETA**2 * momentum) / lead
     ahead_x = gather_ring(over_x, ahead, "x")
-    weights = (up, up_other, down, down_other)
-    near = expert((*own_x, *behind_x, *ahead_x), weights, ((1, 2), (0,)))
-    over_x.hold(11, near[0])
-    over_x.hold(12, rest.done[2])
-    far_x = gather_ring(over_x, far, "x")
-    stay, prev, nxt, far = near[:4]
-    pair = arrived(stay, scatter_ring(over_x, prev, nxt, far, "x"))
-    over_x.depth = 3
-    stay, prev, nxt, far = expert(far_x, weights, ((0,),))
-    far = arrived(stay, scatter_ring(over_x, prev, nxt, far, "x"))
-    back_z = Lane(2)
-    from_ahead = back_z.ring(pair[:CAP].astype(BF16), "zh", -1)
-    passing = back_z.ring(far.astype(BF16), "zh", 1)
-    from_behind = back_z.ring((pair[CAP:] + passing.astype(F32)).astype(BF16), "zh", 1)
-    stay, prev, nxt, far = near[4:]
-    got_x = scatter_ring(over_x, prev, nxt, far, "x")
-    input_grad = place(ids, gate_share, stay, *got_x, from_ahead, from_behind)
+    keep_p, prev_p, next_p, far_p = near[:4]
+    keep_o, prev_o, next_o, far_o = near[4:]
+    keep_a, prev_a, next_a, far_a = expert(ahead_x, weights, ((0,),), (BF16,))
+
+    sent = [hop(far_p, "x", 2), mirrored(prev_p, "x", -1), mirrored(next_p, "x", 1)]
+    pair = keep_p + sum(part.astype(F32) for part in after_all(sent, keep_a))
+    last_sent = [hop(far_a, "x", 2), mirrored(prev_a, "x", -1), mirrored(next_a, "x", 1)]
+    last = keep_a + sum(part.astype(F32) for part in last_sent)
+    far_o, prev_o = after_all((far_o, prev_o), far_a)
+    own_pass, own_got = mirrored(far_o, "x", 1), mirrored(prev_o, "x", -1)
+    own_end = mirrored(joined(next_o, own_pass), "x", 1)
+    from_far = hop(pair[CAP:].astype(BF16), "zh", 2)
+    from_ahead = mirrored(pair[:CAP].astype(BF16), "zh", -1)
+    from_behind = mirrored(last.astype(BF16), "zh", 1)
+    input_grad = place(ids, gate_share, keep_o, own_got, own_end, from_ahead, from_behind, from_far)
     return input_grad[None], new_outer, new_momentum, new_outer.astype(BF16)
 
 

time: 140 us -> 130 us (0.929)
  waiting for transfers between devices: 42.3 us -> 34.1 us
  starting transfers between devices: 57.1 us -> 54.1 us
    ppermute x27 -> x24, waiting for transfers between devices: 41.7 us -> 31.5 us  [mirrored(): return lax.ppermute(value, (axis, 'core'), pairs)]
    ppermute x27 -> x24, starting transfers between devices: 49.8 us -> 43.4 us  [mirrored(): return lax.ppermute(value, (axis, 'core'), pairs)]
    ppermute x2 -> x5, starting transfers between devices: 0.59 us -> 5.49 us  [hop(): lax.ppermute(value, axis, [(i, (i + step) % size) for i in range(size)])]
    ppermute x2 -> x5, waiting for transfers between devices: 0.01 us -> 2.57 us  [hop(): lax.ppermute(value, axis, [(i, (i + step) % size) for i in range(size)])]
    ppermute x3, starting transfers between devices: 6.69 us -> 5.2 us  [swap(): return lax.ppermute(value, (axis, 'core'), pairs)]
    another operation x0 -> x1, other arithmetic: none -> 1.4 us
    unnamed x49 -> x47, local copies, waits for them, and re-layouts: 4.7 us -> 5.9 us
  transfers between devices with their start and end apart: 32 -> 32, of which waited for: 16 -> 12; matrix products, arithmetic and copies ran while one was open for 7% -> 8% of each run, Pallas kernels for 18% -> 19%
where the time goes in v1:
time: 130 us; the launch traced here: 129 us
  starting transfers between devices  54.1 us (42%)
  waiting for transfers between devices  34.1 us (26%)
  Pallas kernels  27 us (21%)
  other arithmetic  6.48 us (5%)
  local copies, waits for them, and re-layouts  5.93 us (5%)
    ppermute x24, starting transfers between devices, mirrored(): return lax.ppermute(value, (axis, 'core'), pairs)  43.4 us
    ppermute x24, waiting for transfers between devices, mirrored(): return lax.ppermute(value, (axis, 'core'), pairs)  31.5 us
    pallas_call x2, Pallas kernels, expert(): pl.pallas_call(functools.partial(expert_kernel, rings), out_shape=tuple((...  20.8 us
    unnamed x47, local copies, waits for them, and re-layouts  5.9 us
    ppermute x5, starting transfers between devices, hop(): lax.ppermute(value, axis, [(i, (i + step) % size) for i in range(size)])  5.49 us
    ppermute x3, starting transfers between devices, swap(): return lax.ppermute(value, (axis, 'core'), pairs)  5.2 us
    pallas_call x1, Pallas kernels, pick(): pl.pallas_call(pick_kernel, out_shape=jax.ShapeDtypeStruct((2 * CAP, widt...  3.54 us
    pallas_call x1, Pallas kernels, place(): pl.pallas_call(place_kernel, grid=(3,), out_shape=jax.ShapeDtypeStruct((c...  2.68 us
  transfers between devices with their start and end apart: 32, of which 12 were waited for; matrix products, arithmetic and copies ran while one was open for 8% of the time, Pallas kernels for 19%

profile of v1, /device:TPU:6, one launch (start us, length us, event | category | flops | bytes accessed | tf_op | source)
XLA Modules:
  0.0 128.5 jit_solution(18412369463321833077)
XLA Ops:
  1.2 3.5 %pick.1.refs_0_ = bf16[32,6144]{1,0:T(8,128)(2,1)} custom-call(s32[2,128]{1,0:T(2,128)} %bitcast.14, bf16[128,6144]{1,0:T(8,128)(2,1)} %bitcast.23, bf16[128,6144]{1,0:T(8,128)(2,1)} %bitcast.24), custom_call_target="tpu_custom_call" | custom-call | flops 50331648 | bytes 3145728 | tf_op jit(solution)/shard_map/pick/pallas_call | solution.py:80
  4.8 2.3 %collective-permute-start = (bf16[32,6144]{1,0:T(8,128)(2,1)}, bf16[32,6144]{1,0:T(8,128)(2,1)}, u32[]{:S(2)}, u32[]{:S(2)}) collective-permute-start(bf16[32,6144]{1,0:T(8,128)(2,1)} %pick.1.refs_0_), channel_id=1, source_target_pairs={{0,8},{1,25},{8,16},{9,1},{16,24},{17,9},{24,0},{25,17},{2,10},{3,... | collective-permute-start | bytes 1179656 | tf_op jit(solution)/shard_map/ppermute | solution.py:29
  10.2 2.8 %collective-permute-done.refs_1_ = bf16[32,6144]{1,0:T(8,128)(2,1)} collective-permute-done((bf16[32,6144]{1,0:T(8,128)(2,1)}, bf16[32,6144]{1,0:T(8,128)(2,1)}, u32[]{:S(2)}, u32[]{:S(2)}) %collective-permute-start) | collective-permute-done | bytes 393248 | tf_op jit(solution)/shard_map/ppermute | solution.py:29
  13.0 3.4 %collective-permute-start.2 = (bf16[32,6144]{1,0:T(8,128)(2,1)}, bf16[32,6144]{1,0:T(8,128)(2,1)}, u32[]{:S(2)}, u32[]{:S(2)}) collective-permute-start(bf16[32,6144]{1,0:T(8,128)(2,1)} %collective-permute-done.refs_1_), channel_id=1, source_target_pairs={{0,8},{1,25},{8,16},{9,1},{16,24},{17,9},{24,0},{25,17},{2,10},{3,... | collective-permute-start | bytes 1179656 | tf_op jit(solution)/shard_map/ppermute | solution.py:29
  16.4 2.9 %collective-permute-done.3.refs_4_ = bf16[32,6144]{1,0:T(8,128)(2,1)} collective-permute-done((bf16[32,6144]{1,0:T(8,128)(2,1)}, bf16[32,6144]{1,0:T(8,128)(2,1)}, u32[]{:S(2)}, u32[]{:S(2)}) %collective-permute-start.3) | collective-permute-done | bytes 393248 | tf_op jit(solution)/shard_map/ppermute | solution.py:29
  21.6 2.0 %copy.13 = f32[1,192,512]{1,2,0:T(8,128)} copy(f32[1,192,512]{2,1,0:T(8,128)} %param.15) | data formatting | bytes 786432 | tf_op args[6]
  23.5 5.4 %collective-permute-start.9 = (bf16[32,6144]{1,0:T(8,128)(2,1)}, bf16[32,6144]{1,0:T(8,128)(2,1)S(1)}, u32[]{:S(2)}, u32[]{:S(2)}) collective-permute-start(bf16[32,6144]{1,0:T(8,128)(2,1)} %collective-permute-done.3.refs_4_), channel_id=1, source_target_pairs={{0,2},{1,7},{2,4},{3,1},{4,6},{5,3},{6,0},{7,5},{8,10},{9,15},{10,... | collective-permute-start | bytes 1179656 | tf_op jit(solution)/shard_map/ppermute | solution.py:29
  32.7 3.1 %collective-permute-start.8 = (bf16[32,6144]{1,0:T(8,128)(2,1)}, bf16[32,6144]{1,0:T(8,128)(2,1)S(1)}, u32[]{:S(2)}, u32[]{:S(2)}) collective-permute-start(bf16[32,6144]{1,0:T(8,128)(2,1)} %collective-permute-done.5.refs_5_), channel_id=1, source_target_pairs={{0,8},{1,25},{8,16},{9,1},{16,24},{17,9},{24,0},{25,17},{2,10},{3,... | collective-permute-start | bytes 1179656 | tf_op jit(solution)/shard_map/ppermute | solution.py:29
  35.9 3.5 %collective-permute-done.9.refs_8_ = bf16[32,6144]{1,0:T(8,128)(2,1)S(1)} collective-permute-done((bf16[32,6144]{1,0:T(8,128)(2,1)}, bf16[32,6144]{1,0:T(8,128)(2,1)S(1)}, u32[]{:S(2)}, u32[]{:S(2)}) %collective-permute-start.9) | collective-permute-done | bytes 393248 | tf_op jit(solution)/shard_map/ppermute | solution.py:29
  41.0 3.1 %collective-permute-start.15 = (f32[192,512]{0,1:T(8,128)S(1)}, f32[192,512]{0,1:T(8,128)S(1)}, u32[]{:S(2)}, u32[]{:S(2)}) collective-permute-start(f32[192,512]{0,1:T(8,128)S(1)} %add.49), channel_id=1, source_target_pairs={{0,96},{1,33},{32,64},{33,1},{64,32},{65,97},{96,0},{97,65},{2,98}... | collective-permute-start | bytes 1179656 | tf_op jit(solution)/shard_map/ppermute | solution.py:267
  44.1 2.9 %collective-permute-start.14 = (bf16[32,6144]{1,0:T(8,128)(2,1)S(1)}, bf16[32,6144]{1,0:T(8,128)(2,1)}, u32[]{:S(2)}, u32[]{:S(2)}) collective-permute-start(bf16[32,6144]{1,0:T(8,128)(2,1)S(1)} %copy-done.6), channel_id=1, source_target_pairs={{0,6},{1,3},{2,0},{3,5},{4,2},{5,7},{6,4},{7,1},{8,14},{9,11},{10,... | collective-permute-start | bytes 1179656 | tf_op jit(solution)/shard_map/ppermute | solution.py:29
  48.5 3.7 %collective-permute-start.13 = (bf16[32,6144]{1,0:T(8,128)(2,1)S(1)}, bf16[32,6144]{1,0:T(8,128)(2,1)S(1)}, u32[]{:S(2)}, u32[]{:S(2)}) collective-permute-start(bf16[32,6144]{1,0:T(8,128)(2,1)S(1)} %collective-permute-done.10.refs_9_), channel_id=1, source_target_pairs={{0,8},{1,25},{8,16},{9,1},{16,24},{17,9},{24,0},{25,17},{2,10},{3,... | collective-permute-start | bytes 1179656 | tf_op jit(solution)/shard_map/ppermute | solution.py:29
  52.2 5.2 %collective-permute-done.14.refs_0_ = bf16[32,6144]{1,0:T(8,128)(2,1)} collective-permute-done((bf16[32,6144]{1,0:T(8,128)(2,1)S(1)}, bf16[32,6144]{1,0:T(8,128)(2,1)}, u32[]{:S(2)}, u32[]{:S(2)}) %collective-permute-start.14) | collective-permute-done | bytes 393248 | tf_op jit(solution)/shard_map/ppermute | solution.py:29
  57.5 2.8 %collective-permute-done.12.refs_10_ = bf16[32,6144]{1,0:T(8,128)(2,1)S(1)} collective-permute-done((bf16[32,6144]{1,0:T(8,128)(2,1)S(1)}, bf16[32,6144]{1,0:T(8,128)(2,1)S(1)}, u32[]{:S(2)}, u32[]{:S(2)}) %collective-permute-start.12) | collective-permute-done | bytes 393248 | tf_op jit(solution)/shard_map/ppermute | solution.py:29
  63.5 10.9 %expert.2 = (f32[32,6144]{1,0:T(8,128)}, bf16[32,6144]{1,0:T(8,128)(2,1)}, bf16[32,6144]{1,0:T(8,128)(2,1)}, bf16[32,6144]{1,0:T(8,128)(2,1)}, f32[16,6144]{1,0:...) custom-call(bf16[32,6144]{1,0:T(8,128)(2,1)} %pick.1.refs_0_, ...), custom_call_target="tpu_custom_call" | custom-call | flops 3623878656 | bytes 25165824 | tf_op jit(solution)/shard_map/expert/pallas_call | solution.py:174
  77.0 2.9 %collective-permute-start.24 = (bf16[32,6144]{1,0:T(8,128)(2,1)}, bf16[32,6144]{1,0:T(8,128)(2,1)}, u32[]{:S(2)}, u32[]{:S(2)}) collective-permute-start(bf16[32,6144]{1,0:T(8,128)(2,1)} %get-tuple-element.61), channel_id=1, source_target_pairs={{0,8},{1,25},{8,16},{9,1},{16,24},{17,9},{24,0},{25,17},{2,10},{3,... | collective-permute-start | bytes 1179656 | tf_op jit(solution)/shard_map/ppermute | solution.py:29
  83.4 7.3 %collective-permute-done.18.refs_3_ = bf16[32,6144]{1,0:T(8,128)(2,1)S(1)} collective-permute-done((bf16[32,6144]{1,0:T(8,128)(2,1)S(1)}, bf16[32,6144]{1,0:T(8,128)(2,1)S(1)}, u32[]{:S(2)}, u32[]{:S(2)}) %collective-permute-start.18) | collective-permute-done | bytes 393248 | tf_op jit(solution)/shard_map/ppermute | solution.py:29
  91.5 9.8 %expert.3 = (f32[16,6144]{1,0:T(8,128)}, bf16[16,6144]{1,0:T(8,128)(2,1)}, bf16[16,6144]{1,0:T(8,128)(2,1)}, bf16[16,6144]{1,0:T(8,128)(2,1)}) custom-call(bf16[32,6144]{1,0:T(8,128)(2,1)} %collective-permute-done.14.refs_0_, bf16[32,6144]{1,0:T(8,128)(2,1)} %copy-done.8, bf16[32,6144]{1,0:T(8,128)(2,1)} %collective-permute-done.17.refs_2_, ...), custom_call_target="tpu_custom_call" | custom-call | flops 1207959552 | bytes 25165824 | tf_op jit(solution)/shard_map/expert/pallas_call | solution.py:174
  101.4 2.9 %collective-permute-start.26 = (bf16[16,6144]{1,0:T(8,128)(2,1)}, bf16[16,6144]{1,0:T(8,128)(2,1)S(1)}, u32[]{:S(2)}, u32[]{:S(2)}) collective-permute-start(bf16[16,6144]{1,0:T(8,128)(2,1)} %get-tuple-element.55), channel_id=1, source_target_pairs={{0,16},{8,24},{16,0},{24,8},{1,17},{9,25},{17,1},{25,9},{2,18},{10... | collective-permute-start | bytes 589832 | tf_op jit(solution)/shard_map/ppermute | solution.py:20
  114.7 2.0 %collective-permute-done.20 = bf16[16,6144]{1,0:T(8,128)(2,1)S(1)} collective-permute-done((bf16[16,6144]{1,0:T(8,128)(2,1)S(1)}, bf16[16,6144]{1,0:T(8,128)(2,1)S(1)}, u32[]{:S(2)}, u32[]{:S(2)}) %collective-permute-start.20) | collective-permute-done | bytes 196640 | tf_op jit(solution)/shard_map/ppermute | solution.py:29
  116.7 3.6 %collective-permute-start.21 = (bf16[16,6144]{1,0:T(8,128)(2,1)S(1)}, bf16[16,6144]{1,0:T(8,128)(2,1)S(1)}, u32[]{:S(2)}, u32[]{:S(2)}) collective-permute-start(bf16[16,6144]{1,0:T(8,128)(2,1)S(1)} %add_convert_fusion.2), channel_id=1, source_target_pairs={{0,8},{1,25},{8,16},{9,1},{16,24},{17,9},{24,0},{25,17},{2,10},{3,... | collective-permute-start | bytes 589832 | tf_op jit(solution)/shard_map/ppermute | solution.py:29
  121.0 2.4 %collective-permute-done.30.refs_4_ = bf16[16,6144]{1,0:T(8,128)(2,1)S(1)} collective-permute-done((bf16[16,6144]{1,0:T(8,128)(2,1)S(1)}, bf16[16,6144]{1,0:T(8,128)(2,1)S(1)}, u32[]{:S(2)}, u32[]{:S(2)}) %collective-permute-start.30) | collective-permute-done | bytes 196640 | tf_op jit(solution)/shard_map/ppermute | solution.py:20
  123.4 2.4 %collective-permute-done.29.refs_3_ = bf16[16,6144]{1,0:T(8,128)(2,1)S(1)} collective-permute-done((bf16[16,6144]{1,0:T(8,128)(2,1)S(1)}, bf16[16,6144]{1,0:T(8,128)(2,1)S(1)}, u32[]{:S(2)}, u32[]{:S(2)}) %collective-permute-start.29) | collective-permute-done | bytes 196640 | tf_op jit(solution)/shard_map/ppermute | solution.py:29
  125.8 2.7 %place.1 = bf16[128,6144]{1,0:T(8,128)(2,1)} custom-call(s32[2,128]{1,0:T(2,128)S(1)} %bitcast.15, f32[1,128]{1,0:T(1,128)S(1)} %copy-done.2, f32[16,6144]{1,0:T(8,128)S(1)} %copy-done, bf16[16,6144]{1,0:T(8,128)(2,1)S(1)} %collective-permute-done.19.refs_0_, bf16[16,6144]{1,0:T(8,128)(2,1)S(1)} %collective-permute-done.21.refs_1_, ...), custom_call_target="tpu_custom_call" | custom-call | flops 25165824 | bytes 1572864 | tf_op jit(solution)/shard_map/place/pallas_call | solution.py:251
  (104 shorter events, 34.0 us)
Async XLA Ops:
  0.6 18.7 %collective-permute-start.4 = (bf16[6144,256]{1,0:T(8,128)(2,1)}, bf16[6144,256]{1,0:T(8,128)(2,1)S(1)}, u32[]{:S(2)}, u32[]{:S(2)}) collective-permute-start(bf16[6144,256]{1,0:T(8,128)(2,1)} %bitcast.16), channel_id=1, source_target_pairs={{0,1},{1,0},{2,3},{3,2},{4,5},{5,4},{6,7},{7,6},{8,9},{9,8},{10,11... | collective-permute-start | bytes 9437192 | tf_op jit(solution)/shard_map/ppermute | solution.py:20
  0.7 28.2 %collective-permute-start.6 = (bf16[256,6144]{1,0:T(8,128)(2,1)}, bf16[256,6144]{1,0:T(8,128)(2,1)}, u32[]{:S(2)}, u32[]{:S(2)}) collective-permute-start(bf16[256,6144]{1,0:T(8,128)(2,1)} %bitcast.19), channel_id=1, source_target_pairs={{0,1},{1,0},{2,3},{3,2},{4,5},{5,4},{6,7},{7,6},{8,9},{9,8},{10,11... | collective-permute-start | bytes 9437192 | tf_op jit(solution)/shard_map/ppermute | solution.py:20
  7.1 12.2 %collective-permute-start.3 = (bf16[32,6144]{1,0:T(8,128)(2,1)}, bf16[32,6144]{1,0:T(8,128)(2,1)}, u32[]{:S(2)}, u32[]{:S(2)}) collective-permute-start(bf16[32,6144]{1,0:T(8,128)(2,1)} %pick.1.refs_0_), channel_id=1, source_target_pairs={{0,2},{1,7},{2,4},{3,1},{4,6},{5,3},{6,0},{7,5},{8,10},{9,15},{10,... | collective-permute-start | bytes 1179656 | tf_op jit(solution)/shard_map/ppermute | solution.py:29
  8.6 10.7 %collective-permute-start.1 = (bf16[32,6144]{1,0:T(8,128)(2,1)}, bf16[32,6144]{1,0:T(8,128)(2,1)S(1)}, u32[]{:S(2)}, u32[]{:S(2)}) collective-permute-start(bf16[32,6144]{1,0:T(8,128)(2,1)} %pick.1.refs_0_), channel_id=1, source_target_pairs={{0,24},{1,9},{8,0},{9,17},{16,8},{17,25},{24,16},{25,1},{2,26},{3,... | collective-permute-start | bytes 1179656 | tf_op jit(solution)/shard_map/ppermute | solution.py:29
  13.0 16.0 %collective-permute-start.2 = (bf16[32,6144]{1,0:T(8,128)(2,1)}, bf16[32,6144]{1,0:T(8,128)(2,1)}, u32[]{:S(2)}, u32[]{:S(2)}) collective-permute-start(bf16[32,6144]{1,0:T(8,128)(2,1)} %collective-permute-done.refs_1_), channel_id=1, source_target_pairs={{0,8},{1,25},{8,16},{9,1},{16,24},{17,9},{24,0},{25,17},{2,10},{3,... | collective-permute-start | bytes 1179656 | tf_op jit(solution)/shard_map/ppermute | solution.py:29
  20.1 12.7 %collective-permute-start.5 = (bf16[32,6144]{1,0:T(8,128)(2,1)}, bf16[32,6144]{1,0:T(8,128)(2,1)}, u32[]{:S(2)}, u32[]{:S(2)}) collective-permute-start(bf16[32,6144]{1,0:T(8,128)(2,1)} %collective-permute-done.3.refs_4_), channel_id=1, source_target_pairs={{0,8},{1,25},{8,16},{9,1},{16,24},{17,9},{24,0},{25,17},{2,10},{3,... | collective-permute-start | bytes 1179656 | tf_op jit(solution)/shard_map/ppermute | solution.py:29
  23.5 15.8 %collective-permute-start.9 = (bf16[32,6144]{1,0:T(8,128)(2,1)}, bf16[32,6144]{1,0:T(8,128)(2,1)S(1)}, u32[]{:S(2)}, u32[]{:S(2)}) collective-permute-start(bf16[32,6144]{1,0:T(8,128)(2,1)} %collective-permute-done.3.refs_4_), channel_id=1, source_target_pairs={{0,2},{1,7},{2,4},{3,1},{4,6},{5,3},{6,0},{7,5},{8,10},{9,15},{10,... | collective-permute-start | bytes 1179656 | tf_op jit(solution)/shard_map/ppermute | solution.py:29
  28.9 10.4 %collective-permute-start.7 = (bf16[32,6144]{1,0:T(8,128)(2,1)}, bf16[32,6144]{1,0:T(8,128)(2,1)S(1)}, u32[]{:S(2)}, u32[]{:S(2)}) collective-permute-start(bf16[32,6144]{1,0:T(8,128)(2,1)} %collective-permute-done.3.refs_4_), channel_id=1, source_target_pairs={{0,24},{1,9},{8,0},{9,17},{16,8},{17,25},{24,16},{25,1},{2,26},{3,... | collective-permute-start | bytes 1179656 | tf_op jit(solution)/shard_map/ppermute | solution.py:29
  32.7 14.3 %collective-permute-start.8 = (bf16[32,6144]{1,0:T(8,128)(2,1)}, bf16[32,6144]{1,0:T(8,128)(2,1)S(1)}, u32[]{:S(2)}, u32[]{:S(2)}) collective-permute-start(bf16[32,6144]{1,0:T(8,128)(2,1)} %collective-permute-done.5.refs_5_), channel_id=1, source_target_pairs={{0,8},{1,25},{8,16},{9,1},{16,24},{17,9},{24,0},{25,17},{2,10},{3,... | collective-permute-start | bytes 1179656 | tf_op jit(solution)/shard_map/ppermute | solution.py:29
  41.0 11.2 %collective-permute-start.15 = (f32[192,512]{0,1:T(8,128)S(1)}, f32[192,512]{0,1:T(8,128)S(1)}, u32[]{:S(2)}, u32[]{:S(2)}) collective-permute-start(f32[192,512]{0,1:T(8,128)S(1)} %add.49), channel_id=1, source_target_pairs={{0,96},{1,33},{32,64},{33,1},{64,32},{65,97},{96,0},{97,65},{2,98}... | collective-permute-start | bytes 1179656 | tf_op jit(solution)/shard_map/ppermute | solution.py:267
  44.1 13.3 %collective-permute-start.14 = (bf16[32,6144]{1,0:T(8,128)(2,1)S(1)}, bf16[32,6144]{1,0:T(8,128)(2,1)}, u32[]{:S(2)}, u32[]{:S(2)}) collective-permute-start(bf16[32,6144]{1,0:T(8,128)(2,1)S(1)} %copy-done.6), channel_id=1, source_target_pairs={{0,6},{1,3},{2,0},{3,5},{4,2},{5,7},{6,4},{7,1},{8,14},{9,11},{10,... | collective-permute-start | bytes 1179656 | tf_op jit(solution)/shard_map/ppermute | solution.py:29
  47.0 13.2 %collective-permute-start.12 = (bf16[32,6144]{1,0:T(8,128)(2,1)S(1)}, bf16[32,6144]{1,0:T(8,128)(2,1)S(1)}, u32[]{:S(2)}, u32[]{:S(2)}) collective-permute-start(bf16[32,6144]{1,0:T(8,128)(2,1)S(1)} %collective-permute-done.9.refs_8_), channel_id=1, source_target_pairs={{0,24},{1,9},{8,0},{9,17},{16,8},{17,25},{24,16},{25,1},{2,26},{3,... | collective-permute-start | bytes 1179656 | tf_op jit(solution)/shard_map/ppermute | solution.py:29
  48.5 12.2 %collective-permute-start.13 = (bf16[32,6144]{1,0:T(8,128)(2,1)S(1)}, bf16[32,6144]{1,0:T(8,128)(2,1)S(1)}, u32[]{:S(2)}, u32[]{:S(2)}) collective-permute-start(bf16[32,6144]{1,0:T(8,128)(2,1)S(1)} %collective-permute-done.10.refs_9_), channel_id=1, source_target_pairs={{0,8},{1,25},{8,16},{9,1},{16,24},{17,9},{24,0},{25,17},{2,10},{3,... | collective-permute-start | bytes 1179656 | tf_op jit(solution)/shard_map/ppermute | solution.py:29
  60.2 14.3 %collective-permute-start.16 = (bf16[32,6144]{1,0:T(8,128)(2,1)}, bf16[32,6144]{1,0:T(8,128)(2,1)S(1)}, u32[]{:S(2)}, u32[]{:S(2)}) collective-permute-start(bf16[32,6144]{1,0:T(8,128)(2,1)} %collective-permute-done.14.refs_0_), channel_id=1, source_target_pairs={{0,8},{1,25},{8,16},{9,1},{16,24},{17,9},{24,0},{25,17},{2,10},{3,... | collective-permute-start | bytes 1179656 | tf_op jit(solution)/shard_map/ppermute | solution.py:29
  60.3 16.6 %collective-permute-start.31 = (f32[192,512]{0,1:T(8,128)S(1)}, f32[192,512]{0,1:T(8,128)}, u32[]{:S(2)}, u32[]{:S(2)}) collective-permute-start(f32[192,512]{0,1:T(8,128)S(1)} %add.57), channel_id=1, source_target_pairs={{0,128},{1,129},{128,0},{129,1},{2,130},{3,131},{130,2},{131,3},{4... | collective-permute-start | bytes 1179656 | tf_op jit(solution)/shard_map/ppermute | solution.py:267
  61.7 21.7 %collective-permute-start.17 = (bf16[32,6144]{1,0:T(8,128)(2,1)}, bf16[32,6144]{1,0:T(8,128)(2,1)}, u32[]{:S(2)}, u32[]{:S(2)}) collective-permute-start(bf16[32,6144]{1,0:T(8,128)(2,1)} %collective-permute-done.14.refs_0_), channel_id=1, source_target_pairs={{0,24},{1,9},{8,0},{9,17},{16,8},{17,25},{24,16},{25,1},{2,26},{3,... | collective-permute-start | bytes 1179656 | tf_op jit(solution)/shard_map/ppermute | solution.py:29
  74.5 16.2 %collective-permute-start.18 = (bf16[32,6144]{1,0:T(8,128)(2,1)S(1)}, bf16[32,6144]{1,0:T(8,128)(2,1)S(1)}, u32[]{:S(2)}, u32[]{:S(2)}) collective-permute-start(bf16[32,6144]{1,0:T(8,128)(2,1)S(1)} %collective-permute-done.16.refs_1_), channel_id=1, source_target_pairs={{0,8},{1,25},{8,16},{9,1},{16,24},{17,9},{24,0},{25,17},{2,10},{3,... | collective-permute-start | bytes 1179656 | tf_op jit(solution)/shard_map/ppermute | solution.py:29
  76.0 30.2 %collective-permute-start.22 = (bf16[32,6144]{1,0:T(8,128)(2,1)}, bf16[32,6144]{1,0:T(8,128)(2,1)}, u32[]{:S(2)}, u32[]{:S(2)}) collective-permute-start(bf16[32,6144]{1,0:T(8,128)(2,1)} %get-tuple-element.59), channel_id=1, source_target_pairs={{0,16},{8,24},{16,0},{24,8},{1,17},{9,25},{17,1},{25,9},{2,18},{10... | collective-permute-start | bytes 1179656 | tf_op jit(solution)/shard_map/ppermute | solution.py:20
  76.6 31.2 %collective-permute-start.23 = (bf16[32,6144]{1,0:T(8,128)(2,1)}, bf16[32,6144]{1,0:T(8,128)(2,1)}, u32[]{:S(2)}, u32[]{:S(2)}) collective-permute-start(bf16[32,6144]{1,0:T(8,128)(2,1)} %get-tuple-element.60), channel_id=1, source_target_pairs={{0,24},{1,9},{8,0},{9,17},{16,8},{17,25},{24,16},{25,1},{2,26},{3,... | collective-permute-start | bytes 1179656 | tf_op jit(solution)/shard_map/ppermute | solution.py:29
  77.0 30.9 %collective-permute-start.24 = (bf16[32,6144]{1,0:T(8,128)(2,1)}, bf16[32,6144]{1,0:T(8,128)(2,1)}, u32[]{:S(2)}, u32[]{:S(2)}) collective-permute-start(bf16[32,6144]{1,0:T(8,128)(2,1)} %get-tuple-element.61), channel_id=1, source_target_pairs={{0,8},{1,25},{8,16},{9,1},{16,24},{17,9},{24,0},{25,17},{2,10},{3,... | collective-permute-start | bytes 1179656 | tf_op jit(solution)/shard_map/ppermute | solution.py:29
  104.3 10.2 %collective-permute-start.27 = (bf16[16,6144]{1,0:T(8,128)(2,1)}, bf16[16,6144]{1,0:T(8,128)(2,1)S(1)}, u32[]{:S(2)}, u32[]{:S(2)}) collective-permute-start(bf16[16,6144]{1,0:T(8,128)(2,1)} %get-tuple-element.66), channel_id=1, source_target_pairs={{0,24},{1,9},{8,0},{9,17},{16,8},{17,25},{24,16},{25,1},{2,26},{3,... | collective-permute-start | bytes 589832 | tf_op jit(solution)/shard_map/ppermute | solution.py:29
  109.3 11.7 %collective-permute-start.25 = (bf16[16,6144]{1,0:T(8,128)(2,1)S(1)}, bf16[16,6144]{1,0:T(8,128)(2,1)S(1)}, u32[]{:S(2)}, u32[]{:S(2)}) collective-permute-start(bf16[16,6144]{1,0:T(8,128)(2,1)S(1)} %get-tuple-element.77), channel_id=1, source_target_pairs={{0,6},{1,3},{2,0},{3,5},{4,2},{5,7},{6,4},{7,1},{8,14},{9,11},{10,... | collective-permute-start | bytes 589832 | tf_op jit(solution)/shard_map/ppermute | solution.py:29
  109.4 14.0 %collective-permute-start.30 = (bf16[16,6144]{1,0:T(8,128)(2,1)S(1)}, bf16[16,6144]{1,0:T(8,128)(2,1)S(1)}, u32[]{:S(2)}, u32[]{:S(2)}) collective-permute-start(bf16[16,6144]{1,0:T(8,128)(2,1)S(1)} %get-tuple-element.76), channel_id=1, source_target_pairs={{0,4},{2,6},{4,0},{6,2},{1,5},{3,7},{5,1},{7,3},{8,12},{10,14},{12... | collective-permute-start | bytes 589832 | tf_op jit(solution)/shard_map/ppermute | solution.py:20
  114.6 11.2 %collective-permute-start.29 = (bf16[16,6144]{1,0:T(8,128)(2,1)S(1)}, bf16[16,6144]{1,0:T(8,128)(2,1)S(1)}, u32[]{:S(2)}, u32[]{:S(2)}) collective-permute-start(bf16[16,6144]{1,0:T(8,128)(2,1)S(1)} %add_convert_fusion.1), channel_id=1, source_target_pairs={{0,2},{1,7},{2,4},{3,1},{4,6},{5,3},{6,0},{7,5},{8,10},{9,15},{10,... | collective-permute-start | bytes 589832 | tf_op jit(solution)/shard_map/ppermute | solution.py:29
  (30 other events, 420.3 us)

commit v2 on v1

--- a/solution.py
+++ b/solution.py
@@ -93,29 +93,26 @@
     )(ids, tokens, grads)
 
 
-CHUNK = 1024
-WIDE = 2 * CHUNK
-
-
-def expert_kernel(rings, *refs):
+def expert_kernel(rings, chunk, wide, *refs):
     places = sum(len(ring) for ring in rings)
     count, made = 4 * places, 4 * len(rings)
     blocks, (up_a, up_b, down_a, down_b), outs = refs[:count], refs[count : count + 4], refs[count + 4 : count + 4 + made]
     rows_v, up_a_v, up_b_v, down_a_v, down_b_v, *held, row_sems, sems, out_sems = refs[count + 4 + made :]
     width, hidden = up_a.shape
+    per = wide // chunk
     rows_in, copies = [], []
-    for c in range(width // CHUNK):
-        if c % 2 == 0:
-            wide = pl.ds(c * CHUNK, WIDE)
+    for c in range(width // chunk):
+        if c % per == 0:
+            span = pl.ds(c * chunk, wide)
             rows_in.append(
                 [
-                    pltpu.make_async_copy(block.at[:, wide], rows_v.at[i, :, wide], row_sems.at[i, c // 2])
+                    pltpu.make_async_copy(block.at[:, span], rows_v.at[i, :, span], row_sems.at[i, c // per])
                     for i, block in enumerate(blocks)
                 ]
             )
             for copy in rows_in[-1]:
                 copy.start()
-        part = pl.ds(c * CHUNK, CHUNK)
+        part = pl.ds(c * chunk, chunk)
         group = (
             pltpu.make_async_copy(up_a.at[part, :], up_a_v.at[part, :], sems.at[0, c]),
             pltpu.make_async_copy(up_b.at[part, :], up_b_v.at[part, :], sems.at[1, c]),
@@ -126,15 +123,15 @@
             copy.start()
         copies.append(group)
     pre_a = pre_b = back_a = back_b = jnp.zeros((count * CAP, hidden), F32)
-    for c in range(width // CHUNK):
-        part = slice(c * CHUNK, (c + 1) * CHUNK)
-        if c % 2 == 0:
-            for copy in rows_in[c // 2]:
+    for c in range(width // chunk):
+        part = slice(c * chunk, (c + 1) * chunk)
+        if c % per == 0:
+            for copy in rows_in[c // per]:
                 copy.wait()
         for copy in copies[c]:
             copy.wait()
-        ins = rows_v[:, :CAP, part].reshape(count * CAP, CHUNK)
-        grads = rows_v[:, CAP:, part].reshape(count * CAP, CHUNK)
+        ins = rows_v[:, :CAP, part].reshape(count * CAP, chunk)
+        grads = rows_v[:, CAP:, part].reshape(count * CAP, chunk)
         pre_a += jnp.dot(ins, up_a_v[part, :], preferred_element_type=F32)
         pre_b += jnp.dot(ins, up_b_v[part, :], preferred_element_type=F32)
         back_a += nt(grads, down_a_v[:, part])
@@ -146,8 +143,8 @@
 
     grad_a, grad_b = hidden_grad(pre_a, back_a), hidden_grad(pre_b, back_b)
     leaving = []
-    for c in range(width // CHUNK):
-        part = slice(c * CHUNK, (c + 1) * CHUNK)
+    for c in range(width // chunk):
+        part = slice(c * chunk, (c + 1) * chunk)
         sums = nt(grad_a, up_a_v[part, :]) + nt(grad_b, up_b_v[part, :])
         for ring, members in enumerate(rings):
             for x in range(4):
@@ -155,24 +152,24 @@
                 for slot, z in enumerate(members):
                     rows = slice(slot * CAP, (slot + 1) * CAP)
                     held[at][rows, part] = sums[(4 * z + x) * CAP : (4 * z + x + 1) * CAP].astype(held[at].dtype)
-                if c % 2 == 1:
-                    wide = pl.ds((c - 1) * CHUNK, WIDE)
+                if c % per == per - 1:
+                    span = pl.ds((c + 1) * chunk - wide, wide)
                     leaving.append(
-                        pltpu.make_async_copy(held[at].at[:, wide], outs[at].at[:, wide], out_sems.at[at, c // 2])
+                        pltpu.make_async_copy(held[at].at[:, span], outs[at].at[:, span], out_sems.at[at, c // per])
                     )
                     leaving[-1].start()
     for copy in leaving:
         copy.wait()
 
 
-def expert(blocks, weights, rings, added):
+def expert(blocks, weights, rings, added, chunk, wide):
     width, hidden = weights[0].shape
     rows = len(blocks) * CAP
-    anywhere = pl.BlockSpec(memory_space=pl.ANY)
+    anywhere = pl.BlockSpec(memory_space=pltpu.HBM)
     shapes = [(len(members) * CAP, width) for members in rings for _ in range(4)]
     kinds = [kind for third in added for kind in (F32, BF16, third, BF16)]
     return pl.pallas_call(
-        functools.partial(expert_kernel, rings),
+        functools.partial(expert_kernel, rings, chunk, wide),
         out_shape=tuple(jax.ShapeDtypeStruct(shape, kind) for shape, kind in zip(shapes, kinds)),
         in_specs=[anywhere] * (len(blocks) + 4),
         out_specs=(anywhere,) * len(shapes),
@@ -183,9 +180,9 @@
             pltpu.VMEM((hidden, width), BF16),
             pltpu.VMEM((hidden, width), BF16),
             *(pltpu.VMEM(shape, kind) for shape, kind in zip(shapes, kinds)),
-            pltpu.SemaphoreType.DMA((len(blocks), width // WIDE)),
-            pltpu.SemaphoreType.DMA((4, width // CHUNK)),
-            pltpu.SemaphoreType.DMA((len(shapes), width // WIDE)),
+            pltpu.SemaphoreType.DMA((len(blocks), width // wide)),
+            pltpu.SemaphoreType.DMA((4, width // chunk)),
+            pltpu.SemaphoreType.DMA((len(shapes), width // wide)),
         ],
         compiler_params=pltpu.CompilerParams(vmem_limit_bytes=60 * MIB),
         cost_estimate=pl.CostEstimate(
@@ -303,16 +300,16 @@
     behind_x = gather_ring(over_x, behind, "x")
     far_x = gather_ring(over_x, far, "x")
     weights = (up, up_other, down, down_other)
-    near = expert((*own_x, *behind_x, *far_x), weights, ((1, 2), (0,)), (BF16, F32))
-    over_x.hold(11, near[0])
+    near = expert((*own_x, *behind_x, *far_x), weights, ((1, 2), (0,)), (BF16, F32), 1024, 2048)
     step = lead * outer_keys + after(summed, near[0])
     new_outer = outer_keys - OUTER_RATE * step
     share = lax.dynamic_slice_in_dim(step, place_at * width, width, 1)
     new_momentum = OUTER_BETA * momentum + (share - OUTER_BETA**2 * momentum) / lead
-    ahead_x = gather_ring(over_x, ahead, "x")
+    over_x.depth = 3
+    ahead_x = (ahead, over_x.ring(ahead, "x", 1), over_x.ring(ahead, "x", -1), over_x.straight(ahead, "x", 2))
     keep_p, prev_p, next_p, far_p = near[:4]
     keep_o, prev_o, next_o, far_o = near[4:]
-    keep_a, prev_a, next_a, far_a = expert(ahead_x, weights, ((0,),), (BF16,))
+    keep_a, prev_a, next_a, far_a = expert(ahead_x, weights, ((0,),), (BF16,), 1536, 1536)
 
     sent = [hop(far_p, "x", 2), mirrored(prev_p, "x", -1), mirrored(next_p, "x", 1)]
     pair = keep_p + sum(part.astype(F32) for part in after_all(sent, keep_a))

time: 130 us -> 128 us (0.985); the launches traced: 129 us -> 125 us
  waiting for transfers between devices: 34.1 us -> 21.6 us
  starting transfers between devices: 54.1 us -> 64.8 us
    ppermute x24 -> x23, waiting for transfers between devices: 31.5 us -> 21.5 us  [mirrored(): return lax.ppermute(value, (axis, 'core'), pairs)]
    ppermute x5 -> x6, starting transfers between devices: 5.49 us -> 11.3 us  [hop(): lax.ppermute(value, axis, [(i, (i + step) % size) for i in range(size)])]
    ppermute x24 -> x23, starting transfers between devices: 43.4 us -> 46.1 us  [mirrored(): return lax.ppermute(value, (axis, 'core'), pairs)]
    ppermute x5 -> x6, waiting for transfers between devices: 2.57 us -> 0.02 us  [hop(): lax.ppermute(value, axis, [(i, (i + step) % size) for i in range(size)])]
    ppermute x3, starting transfers between devices: 5.2 us -> 7.46 us  [swap(): return lax.ppermute(value, (axis, 'core'), pairs)]
    unnamed x47 -> x39, local copies, waits for them, and re-layouts: 5.9 us -> 4.94 us
  transfers between devices with their start and end apart: 32 -> 32, of which waited for: 12 -> 9; matrix products, arithmetic and copies ran while one was open for 8% -> 8% of each run, Pallas kernels for 19% -> 19%
where the time goes in v2:
time: 128 us; the launch traced here: 125 us
  starting transfers between devices  64.8 us (51%)
  Pallas kernels  26.5 us (21%)
  waiting for transfers between devices  21.6 us (17%)
  other arithmetic  6.23 us (5%)
  local copies, waits for them, and re-layouts  4.97 us (4%)
    ppermute x23, starting transfers between devices, mirrored(): return lax.ppermute(value, (axis, 'core'), pairs)  46.1 us
    ppermute x23, waiting for transfers between devices, mirrored(): return lax.ppermute(value, (axis, 'core'), pairs)  21.5 us
    pallas_call x2, Pallas kernels, expert(): pl.pallas_call(functools.partial(expert_kernel, rings, chunk, wide), out_...  20.3 us
    ppermute x6, starting transfers between devices, hop(): lax.ppermute(value, axis, [(i, (i + step) % size) for i in range(size)])  11.3 us
    ppermute x3, starting transfers between devices, swap(): return lax.ppermute(value, (axis, 'core'), pairs)  7.46 us
    unnamed x39, local copies, waits for them, and re-layouts  4.94 us
    pallas_call x1, Pallas kernels, pick(): pl.pallas_call(pick_kernel, out_shape=jax.ShapeDtypeStruct((2 * CAP, widt...  3.54 us
    pallas_call x1, Pallas kernels, place(): pl.pallas_call(place_kernel, grid=(3,), out_shape=jax.ShapeDtypeStruct((c...  2.68 us
  transfers between devices with their start and end apart: 32, of which 9 were waited for; matrix products, arithmetic and copies ran while one was open for 8% of the time, Pallas kernels for 19%

profile of v2, /device:TPU:6, one launch (start us, length us, event | category | flops | bytes accessed | tf_op | source)
XLA Modules:
  0.0 125.0 jit_solution(13099086472878538539)
XLA Ops:
  1.2 3.5 %pick.1.refs_0_ = bf16[32,6144]{1,0:T(8,128)(2,1)} custom-call(s32[2,128]{1,0:T(2,128)} %bitcast.14, bf16[128,6144]{1,0:T(8,128)(2,1)} %bitcast.23, bf16[128,6144]{1,0:T(8,128)(2,1)} %bitcast.24), custom_call_target="tpu_custom_call" | custom-call | flops 50331648 | bytes 3145728 | tf_op jit(solution)/shard_map/pick/pallas_call | solution.py:80
  4.8 2.3 %collective-permute-start = (bf16[32,6144]{1,0:T(8,128)(2,1)}, bf16[32,6144]{1,0:T(8,128)(2,1)}, u32[]{:S(2)}, u32[]{:S(2)}) collective-permute-start(bf16[32,6144]{1,0:T(8,128)(2,1)} %pick.1.refs_0_), channel_id=1, source_target_pairs={{0,8},{1,25},{8,16},{9,1},{16,24},{17,9},{24,0},{25,17},{2,10},{3,... | collective-permute-start | bytes 1179656 | tf_op jit(solution)/shard_map/ppermute | solution.py:29
  10.2 2.8 %collective-permute-done.refs_1_ = bf16[32,6144]{1,0:T(8,128)(2,1)} collective-permute-done((bf16[32,6144]{1,0:T(8,128)(2,1)}, bf16[32,6144]{1,0:T(8,128)(2,1)}, u32[]{:S(2)}, u32[]{:S(2)}) %collective-permute-start) | collective-permute-done | bytes 393248 | tf_op jit(solution)/shard_map/ppermute | solution.py:29
  13.0 3.4 %collective-permute-start.2 = (bf16[32,6144]{1,0:T(8,128)(2,1)}, bf16[32,6144]{1,0:T(8,128)(2,1)}, u32[]{:S(2)}, u32[]{:S(2)}) collective-permute-start(bf16[32,6144]{1,0:T(8,128)(2,1)} %collective-permute-done.refs_1_), channel_id=1, source_target_pairs={{0,8},{1,25},{8,16},{9,1},{16,24},{17,9},{24,0},{25,17},{2,10},{3,... | collective-permute-start | bytes 1179656 | tf_op jit(solution)/shard_map/ppermute | solution.py:29
  19.3 3.5 %collective-permute-start.9 = (bf16[32,6144]{1,0:T(8,128)(2,1)}, bf16[32,6144]{1,0:T(8,128)(2,1)}, u32[]{:S(2)}, u32[]{:S(2)}) collective-permute-start(bf16[32,6144]{1,0:T(8,128)(2,1)} %collective-permute-done.3.refs_4_), channel_id=1, source_target_pairs={{0,2},{1,7},{2,4},{3,1},{4,6},{5,3},{6,0},{7,5},{8,10},{9,15},{10,... | collective-permute-start | bytes 1179656 | tf_op jit(solution)/shard_map/ppermute | solution.py:29
  28.7 5.3 %collective-permute-done.5.refs_5_ = bf16[32,6144]{1,0:T(8,128)(2,1)} collective-permute-done((bf16[32,6144]{1,0:T(8,128)(2,1)}, bf16[32,6144]{1,0:T(8,128)(2,1)}, u32[]{:S(2)}, u32[]{:S(2)}) %collective-permute-start.5) | collective-permute-done | bytes 393248 | tf_op jit(solution)/shard_map/ppermute | solution.py:29
  35.4 2.0 %collective-permute-done.7.refs_6_ = bf16[32,6144]{1,0:T(8,128)(2,1)} collective-permute-done((bf16[32,6144]{1,0:T(8,128)(2,1)}, bf16[32,6144]{1,0:T(8,128)(2,1)}, u32[]{:S(2)}, u32[]{:S(2)}) %collective-permute-start.7) | collective-permute-done | bytes 393248 | tf_op jit(solution)/shard_map/ppermute | solution.py:29
  38.7 3.1 %collective-permute-start.15 = (f32[192,512]{0,1:T(8,128)S(1)}, f32[192,512]{0,1:T(8,128)S(1)}, u32[]{:S(2)}, u32[]{:S(2)}) collective-permute-start(f32[192,512]{0,1:T(8,128)S(1)} %add.49), channel_id=1, source_target_pairs={{0,96},{1,33},{32,64},{33,1},{64,32},{65,97},{96,0},{97,65},{2,98}... | collective-permute-start | bytes 1179656 | tf_op jit(solution)/shard_map/ppermute | solution.py:264
  41.8 4.6 %collective-permute-start.14 = (bf16[32,6144]{1,0:T(8,128)(2,1)S(1)}, bf16[32,6144]{1,0:T(8,128)(2,1)}, u32[]{:S(2)}, u32[]{:S(2)}) collective-permute-start(bf16[32,6144]{1,0:T(8,128)(2,1)S(1)} %copy-done.6), channel_id=1, source_target_pairs={{0,6},{1,3},{2,0},{3,5},{4,2},{5,7},{6,4},{7,1},{8,14},{9,11},{10,... | collective-permute-start | bytes 1179656 | tf_op jit(solution)/shard_map/ppermute | solution.py:29
  46.4 3.2 %collective-permute-start.13 = (bf16[32,6144]{1,0:T(8,128)(2,1)S(1)}, bf16[32,6144]{1,0:T(8,128)(2,1)S(1)}, u32[]{:S(2)}, u32[]{:S(2)}) collective-permute-start(bf16[32,6144]{1,0:T(8,128)(2,1)S(1)} %collective-permute-done.10.refs_9_), channel_id=1, source_target_pairs={{0,8},{1,25},{8,16},{9,1},{16,24},{17,9},{24,0},{25,17},{2,10},{3,... | collective-permute-start | bytes 1179656 | tf_op jit(solution)/shard_map/ppermute | solution.py:29
  49.7 2.7 %collective-permute-start.31 = (f32[192,512]{0,1:T(8,128)S(1)}, f32[192,512]{0,1:T(8,128)}, u32[]{:S(2)}, u32[]{:S(2)}) collective-permute-start(f32[192,512]{0,1:T(8,128)S(1)} %add.57), channel_id=1, source_target_pairs={{0,128},{1,129},{128,0},{129,1},{2,130},{3,131},{130,2},{131,3},{4... | collective-permute-start | bytes 1179656 | tf_op jit(solution)/shard_map/ppermute | solution.py:264
  54.1 2.5 %collective-permute-start.16 = (bf16[32,6144]{1,0:T(8,128)(2,1)}, bf16[32,6144]{1,0:T(8,128)(2,1)S(1)}, u32[]{:S(2)}, u32[]{:S(2)}) collective-permute-start(bf16[32,6144]{1,0:T(8,128)(2,1)} %collective-permute-done.14.refs_0_), channel_id=1, source_target_pairs={{0,8},{1,25},{8,16},{9,1},{16,24},{17,9},{24,0},{25,17},{2,10},{3,... | collective-permute-start | bytes 1179656 | tf_op jit(solution)/shard_map/ppermute | solution.py:29
  59.2 3.8 %collective-permute-start.18 = (bf16[32,6144]{1,0:T(8,128)(2,1)}, bf16[32,6144]{1,0:T(8,128)(2,1)}, u32[]{:S(2)}, u32[]{:S(2)}) collective-permute-start(bf16[32,6144]{1,0:T(8,128)(2,1)} %collective-permute-done.14.refs_0_), channel_id=1, source_target_pairs={{0,16},{8,24},{16,0},{24,8},{1,17},{9,25},{17,1},{25,9},{2,18},{10... | collective-permute-start | bytes 1179656 | tf_op jit(solution)/shard_map/ppermute | solution.py:20
  63.0 10.9 %expert.2 = (f32[32,6144]{1,0:T(8,128)}, bf16[32,6144]{1,0:T(8,128)(2,1)}, bf16[32,6144]{1,0:T(8,128)(2,1)}, bf16[32,6144]{1,0:T(8,128)(2,1)}, f32[16,6144]{1,0:...) custom-call(bf16[32,6144]{1,0:T(8,128)(2,1)} %pick.1.refs_0_, ...), custom_call_target="tpu_custom_call" | custom-call | flops 3623878656 | bytes 25165824 | tf_op jit(solution)/shard_map/expert/pallas_call | solution.py:171
  75.3 2.0 %collective-permute-start.24 = (bf16[32,6144]{1,0:T(8,128)(2,1)}, bf16[32,6144]{1,0:T(8,128)(2,1)}, u32[]{:S(2)}, u32[]{:S(2)}) collective-permute-start(bf16[32,6144]{1,0:T(8,128)(2,1)} %get-tuple-element.61), channel_id=1, source_target_pairs={{0,8},{1,25},{8,16},{9,1},{16,24},{17,9},{24,0},{25,17},{2,10},{3,... | collective-permute-start | bytes 1179656 | tf_op jit(solution)/shard_map/ppermute | solution.py:29
  80.9 9.4 %expert.3 = (f32[16,6144]{1,0:T(8,128)}, bf16[16,6144]{1,0:T(8,128)(2,1)}, bf16[16,6144]{1,0:T(8,128)(2,1)}, bf16[16,6144]{1,0:T(8,128)(2,1)}) custom-call(bf16[32,6144]{1,0:T(8,128)(2,1)} %collective-permute-done.14.refs_0_, bf16[32,6144]{1,0:T(8,128)(2,1)} %copy-done.8, bf16[32,6144]{1,0:T(8,128)(2,1)} %collective-permute-done.17.refs_2_, ...), custom_call_target="tpu_custom_call" | custom-call | flops 1207959552 | bytes 25165824 | tf_op jit(solution)/shard_map/expert/pallas_call | solution.py:171
  90.3 2.3 %collective-permute-start.26 = (bf16[16,6144]{1,0:T(8,128)(2,1)}, bf16[16,6144]{1,0:T(8,128)(2,1)S(1)}, u32[]{:S(2)}, u32[]{:S(2)}) collective-permute-start(bf16[16,6144]{1,0:T(8,128)(2,1)} %get-tuple-element.54), channel_id=1, source_target_pairs={{0,16},{8,24},{16,0},{24,8},{1,17},{9,25},{17,1},{25,9},{2,18},{10... | collective-permute-start | bytes 589832 | tf_op jit(solution)/shard_map/ppermute | solution.py:20
  92.8 3.1 %collective-permute-start.28 = (bf16[16,6144]{1,0:T(8,128)(2,1)}, bf16[16,6144]{1,0:T(8,128)(2,1)S(1)}, u32[]{:S(2)}, u32[]{:S(2)}) collective-permute-start(bf16[16,6144]{1,0:T(8,128)(2,1)} %get-tuple-element.67), channel_id=1, source_target_pairs={{0,8},{1,25},{8,16},{9,1},{16,24},{17,9},{24,0},{25,17},{2,10},{3,... | collective-permute-start | bytes 589832 | tf_op jit(solution)/shard_map/ppermute | solution.py:29
  97.1 8.6 %collective-permute-start.25 = (bf16[16,6144]{1,0:T(8,128)(2,1)S(1)}, bf16[16,6144]{1,0:T(8,128)(2,1)S(1)}, u32[]{:S(2)}, u32[]{:S(2)}) collective-permute-start(bf16[16,6144]{1,0:T(8,128)(2,1)S(1)} %get-tuple-element.77), channel_id=1, source_target_pairs={{0,6},{1,3},{2,0},{3,5},{4,2},{5,7},{6,4},{7,1},{8,14},{9,11},{10,... | collective-permute-start | bytes 589832 | tf_op jit(solution)/shard_map/ppermute | solution.py:29
  105.8 4.5 %collective-permute-start.30 = (bf16[16,6144]{1,0:T(8,128)(2,1)S(1)}, bf16[16,6144]{1,0:T(8,128)(2,1)S(1)}, u32[]{:S(2)}, u32[]{:S(2)}) collective-permute-start(bf16[16,6144]{1,0:T(8,128)(2,1)S(1)} %get-tuple-element.76), channel_id=1, source_target_pairs={{0,4},{2,6},{4,0},{6,2},{1,5},{3,7},{5,1},{7,3},{8,12},{10,14},{12... | collective-permute-start | bytes 589832 | tf_op jit(solution)/shard_map/ppermute | solution.py:20
  110.3 2.0 %collective-permute-start.19 = (bf16[16,6144]{1,0:T(8,128)(2,1)S(1)}, bf16[16,6144]{1,0:T(8,128)(2,1)S(1)}, u32[]{:S(2)}, u32[]{:S(2)}) collective-permute-start(bf16[16,6144]{1,0:T(8,128)(2,1)S(1)} %copy-done.16), channel_id=1, source_target_pairs={{0,24},{1,9},{8,0},{9,17},{16,8},{17,25},{24,16},{25,1},{2,26},{3,... | collective-permute-start | bytes 589832 | tf_op jit(solution)/shard_map/ppermute | solution.py:29
  112.5 3.4 %collective-permute-done.20 = bf16[16,6144]{1,0:T(8,128)(2,1)S(1)} collective-permute-done((bf16[16,6144]{1,0:T(8,128)(2,1)S(1)}, bf16[16,6144]{1,0:T(8,128)(2,1)S(1)}, u32[]{:S(2)}, u32[]{:S(2)}) %collective-permute-start.20) | collective-permute-done | bytes 196640 | tf_op jit(solution)/shard_map/ppermute | solution.py:29
  118.0 3.7 %collective-permute-done.25.refs_2_ = bf16[16,6144]{1,0:T(8,128)(2,1)S(1)} collective-permute-done((bf16[16,6144]{1,0:T(8,128)(2,1)S(1)}, bf16[16,6144]{1,0:T(8,128)(2,1)S(1)}, u32[]{:S(2)}, u32[]{:S(2)}) %collective-permute-start.25) | collective-permute-done | bytes 196640 | tf_op jit(solution)/shard_map/ppermute | solution.py:29
  122.3 2.7 %place.1 = bf16[128,6144]{1,0:T(8,128)(2,1)} custom-call(s32[2,128]{1,0:T(2,128)S(1)} %bitcast.15, f32[1,128]{1,0:T(1,128)S(1)} %copy-done.2, f32[16,6144]{1,0:T(8,128)S(1)} %copy-done, bf16[16,6144]{1,0:T(8,128)(2,1)S(1)} %collective-permute-done.19.refs_0_, bf16[16,6144]{1,0:T(8,128)(2,1)S(1)} %collective-permute-done.21.refs_1_, ...), custom_call_target="tpu_custom_call" | custom-call | flops 25165824 | bytes 1572864 | tf_op jit(solution)/shard_map/place/pallas_call | solution.py:248
  (96 shorter events, 28.5 us)
Async XLA Ops:
  0.6 22.2 %collective-permute-start.4 = (bf16[6144,256]{1,0:T(8,128)(2,1)}, bf16[6144,256]{1,0:T(8,128)(2,1)S(1)}, u32[]{:S(2)}, u32[]{:S(2)}) collective-permute-start(bf16[6144,256]{1,0:T(8,128)(2,1)} %bitcast.16), channel_id=1, source_target_pairs={{0,1},{1,0},{2,3},{3,2},{4,5},{5,4},{6,7},{7,6},{8,9},{9,8},{10,11... | collective-permute-start | bytes 9437192 | tf_op jit(solution)/shard_map/ppermute | solution.py:20
  0.7 23.7 %collective-permute-start.6 = (bf16[256,6144]{1,0:T(8,128)(2,1)}, bf16[256,6144]{1,0:T(8,128)(2,1)}, u32[]{:S(2)}, u32[]{:S(2)}) collective-permute-start(bf16[256,6144]{1,0:T(8,128)(2,1)} %bitcast.19), channel_id=1, source_target_pairs={{0,1},{1,0},{2,3},{3,2},{4,5},{5,4},{6,7},{7,6},{8,9},{9,8},{10,11... | collective-permute-start | bytes 9437192 | tf_op jit(solution)/shard_map/ppermute | solution.py:20
  7.1 12.2 %collective-permute-start.3 = (bf16[32,6144]{1,0:T(8,128)(2,1)}, bf16[32,6144]{1,0:T(8,128)(2,1)}, u32[]{:S(2)}, u32[]{:S(2)}) collective-permute-start(bf16[32,6144]{1,0:T(8,128)(2,1)} %pick.1.refs_0_), channel_id=1, source_target_pairs={{0,2},{1,7},{2,4},{3,1},{4,6},{5,3},{6,0},{7,5},{8,10},{9,15},{10,... | collective-permute-start | bytes 1179656 | tf_op jit(solution)/shard_map/ppermute | solution.py:29
  8.6 14.2 %collective-permute-start.1 = (bf16[32,6144]{1,0:T(8,128)(2,1)}, bf16[32,6144]{1,0:T(8,128)(2,1)}, u32[]{:S(2)}, u32[]{:S(2)}) collective-permute-start(bf16[32,6144]{1,0:T(8,128)(2,1)} %pick.1.refs_0_), channel_id=1, source_target_pairs={{0,24},{1,9},{8,0},{9,17},{16,8},{17,25},{24,16},{25,1},{2,26},{3,... | collective-permute-start | bytes 1179656 | tf_op jit(solution)/shard_map/ppermute | solution.py:29
  13.0 11.5 %collective-permute-start.2 = (bf16[32,6144]{1,0:T(8,128)(2,1)}, bf16[32,6144]{1,0:T(8,128)(2,1)}, u32[]{:S(2)}, u32[]{:S(2)}) collective-permute-start(bf16[32,6144]{1,0:T(8,128)(2,1)} %collective-permute-done.refs_1_), channel_id=1, source_target_pairs={{0,8},{1,25},{8,16},{9,1},{16,24},{17,9},{24,0},{25,17},{2,10},{3,... | collective-permute-start | bytes 1179656 | tf_op jit(solution)/shard_map/ppermute | solution.py:29
  19.3 16.1 %collective-permute-start.9 = (bf16[32,6144]{1,0:T(8,128)(2,1)}, bf16[32,6144]{1,0:T(8,128)(2,1)}, u32[]{:S(2)}, u32[]{:S(2)}) collective-permute-start(bf16[32,6144]{1,0:T(8,128)(2,1)} %collective-permute-done.3.refs_4_), channel_id=1, source_target_pairs={{0,2},{1,7},{2,4},{3,1},{4,6},{5,3},{6,0},{7,5},{8,10},{9,15},{10,... | collective-permute-start | bytes 1179656 | tf_op jit(solution)/shard_map/ppermute | solution.py:29
  24.4 13.0 %collective-permute-start.7 = (bf16[32,6144]{1,0:T(8,128)(2,1)}, bf16[32,6144]{1,0:T(8,128)(2,1)}, u32[]{:S(2)}, u32[]{:S(2)}) collective-permute-start(bf16[32,6144]{1,0:T(8,128)(2,1)} %collective-permute-done.3.refs_4_), channel_id=1, source_target_pairs={{0,24},{1,9},{8,0},{9,17},{16,8},{17,25},{24,16},{25,1},{2,26},{3,... | collective-permute-start | bytes 1179656 | tf_op jit(solution)/shard_map/ppermute | solution.py:29
  27.0 11.7 %collective-permute-start.11 = (f32[192,512]{0,1:T(8,128)S(1)}, f32[192,512]{0,1:T(8,128)S(1)}, u32[]{:S(2)}, u32[]{:S(2)}) collective-permute-start(f32[192,512]{0,1:T(8,128)S(1)} %bitcast_subtract_fusion), channel_id=1, source_target_pairs={{0,32},{1,97},{32,0},{33,65},{64,96},{65,33},{96,64},{97,1},{2,34}... | collective-permute-start | bytes 1179656 | tf_op jit(solution)/shard_map/ppermute | solution.py:264
  33.9 12.5 %collective-permute-start.8 = (bf16[32,6144]{1,0:T(8,128)(2,1)}, bf16[32,6144]{1,0:T(8,128)(2,1)S(1)}, u32[]{:S(2)}, u32[]{:S(2)}) collective-permute-start(bf16[32,6144]{1,0:T(8,128)(2,1)} %collective-permute-done.5.refs_5_), channel_id=1, source_target_pairs={{0,8},{1,25},{8,16},{9,1},{16,24},{17,9},{24,0},{25,17},{2,10},{3,... | collective-permute-start | bytes 1179656 | tf_op jit(solution)/shard_map/ppermute | solution.py:29
  41.8 12.3 %collective-permute-start.14 = (bf16[32,6144]{1,0:T(8,128)(2,1)S(1)}, bf16[32,6144]{1,0:T(8,128)(2,1)}, u32[]{:S(2)}, u32[]{:S(2)}) collective-permute-start(bf16[32,6144]{1,0:T(8,128)(2,1)S(1)} %copy-done.6), channel_id=1, source_target_pairs={{0,6},{1,3},{2,0},{3,5},{4,2},{5,7},{6,4},{7,1},{8,14},{9,11},{10,... | collective-permute-start | bytes 1179656 | tf_op jit(solution)/shard_map/ppermute | solution.py:29
  46.4 11.3 %collective-permute-start.12 = (bf16[32,6144]{1,0:T(8,128)(2,1)}, bf16[32,6144]{1,0:T(8,128)(2,1)S(1)}, u32[]{:S(2)}, u32[]{:S(2)}) collective-permute-start(bf16[32,6144]{1,0:T(8,128)(2,1)} %collective-permute-done.9.refs_8_), channel_id=1, source_target_pairs={{0,24},{1,9},{8,0},{9,17},{16,8},{17,25},{24,16},{25,1},{2,26},{3,... | collective-permute-start | bytes 1179656 | tf_op jit(solution)/shard_map/ppermute | solution.py:29
  49.7 24.3 %collective-permute-start.31 = (f32[192,512]{0,1:T(8,128)S(1)}, f32[192,512]{0,1:T(8,128)}, u32[]{:S(2)}, u32[]{:S(2)}) collective-permute-start(f32[192,512]{0,1:T(8,128)S(1)} %add.57), channel_id=1, source_target_pairs={{0,128},{1,129},{128,0},{129,1},{2,130},{3,131},{130,2},{131,3},{4... | collective-permute-start | bytes 1179656 | tf_op jit(solution)/shard_map/ppermute | solution.py:264
  54.1 21.2 %collective-permute-start.16 = (bf16[32,6144]{1,0:T(8,128)(2,1)}, bf16[32,6144]{1,0:T(8,128)(2,1)S(1)}, u32[]{:S(2)}, u32[]{:S(2)}) collective-permute-start(bf16[32,6144]{1,0:T(8,128)(2,1)} %collective-permute-done.14.refs_0_), channel_id=1, source_target_pairs={{0,8},{1,25},{8,16},{9,1},{16,24},{17,9},{24,0},{25,17},{2,10},{3,... | collective-permute-start | bytes 1179656 | tf_op jit(solution)/shard_map/ppermute | solution.py:29
  57.7 23.2 %collective-permute-start.17 = (bf16[32,6144]{1,0:T(8,128)(2,1)}, bf16[32,6144]{1,0:T(8,128)(2,1)}, u32[]{:S(2)}, u32[]{:S(2)}) collective-permute-start(bf16[32,6144]{1,0:T(8,128)(2,1)} %collective-permute-done.14.refs_0_), channel_id=1, source_target_pairs={{0,24},{1,9},{8,0},{9,17},{16,8},{17,25},{24,16},{25,1},{2,26},{3,... | collective-permute-start | bytes 1179656 | tf_op jit(solution)/shard_map/ppermute | solution.py:29
  59.2 21.7 %collective-permute-start.18 = (bf16[32,6144]{1,0:T(8,128)(2,1)}, bf16[32,6144]{1,0:T(8,128)(2,1)}, u32[]{:S(2)}, u32[]{:S(2)}) collective-permute-start(bf16[32,6144]{1,0:T(8,128)(2,1)} %collective-permute-done.14.refs_0_), channel_id=1, source_target_pairs={{0,16},{8,24},{16,0},{24,8},{1,17},{9,25},{17,1},{25,9},{2,18},{10... | collective-permute-start | bytes 1179656 | tf_op jit(solution)/shard_map/ppermute | solution.py:20
  73.9 18.9 %collective-permute-start.22 = (bf16[32,6144]{1,0:T(8,128)(2,1)}, bf16[32,6144]{1,0:T(8,128)(2,1)S(1)}, u32[]{:S(2)}, u32[]{:S(2)}) collective-permute-start(bf16[32,6144]{1,0:T(8,128)(2,1)} %get-tuple-element.59), channel_id=1, source_target_pairs={{0,16},{8,24},{16,0},{24,8},{1,17},{9,25},{17,1},{25,9},{2,18},{10... | collective-permute-start | bytes 1179656 | tf_op jit(solution)/shard_map/ppermute | solution.py:20
  74.0 21.9 %collective-permute-start.23 = (bf16[32,6144]{1,0:T(8,128)(2,1)}, bf16[32,6144]{1,0:T(8,128)(2,1)S(1)}, u32[]{:S(2)}, u32[]{:S(2)}) collective-permute-start(bf16[32,6144]{1,0:T(8,128)(2,1)} %get-tuple-element.60), channel_id=1, source_target_pairs={{0,24},{1,9},{8,0},{9,17},{16,8},{17,25},{24,16},{25,1},{2,26},{3,... | collective-permute-start | bytes 1179656 | tf_op jit(solution)/shard_map/ppermute | solution.py:29
  75.3 20.6 %collective-permute-start.24 = (bf16[32,6144]{1,0:T(8,128)(2,1)}, bf16[32,6144]{1,0:T(8,128)(2,1)}, u32[]{:S(2)}, u32[]{:S(2)}) collective-permute-start(bf16[32,6144]{1,0:T(8,128)(2,1)} %get-tuple-element.61), channel_id=1, source_target_pairs={{0,8},{1,25},{8,16},{9,1},{16,24},{17,9},{24,0},{25,17},{2,10},{3,... | collective-permute-start | bytes 1179656 | tf_op jit(solution)/shard_map/ppermute | solution.py:29
  90.3 20.0 %collective-permute-start.26 = (bf16[16,6144]{1,0:T(8,128)(2,1)}, bf16[16,6144]{1,0:T(8,128)(2,1)S(1)}, u32[]{:S(2)}, u32[]{:S(2)}) collective-permute-start(bf16[16,6144]{1,0:T(8,128)(2,1)} %get-tuple-element.54), channel_id=1, source_target_pairs={{0,16},{8,24},{16,0},{24,8},{1,17},{9,25},{17,1},{25,9},{2,18},{10... | collective-permute-start | bytes 589832 | tf_op jit(solution)/shard_map/ppermute | solution.py:20
  92.7 17.7 %collective-permute-start.27 = (bf16[16,6144]{1,0:T(8,128)(2,1)}, bf16[16,6144]{1,0:T(8,128)(2,1)S(1)}, u32[]{:S(2)}, u32[]{:S(2)}) collective-permute-start(bf16[16,6144]{1,0:T(8,128)(2,1)} %get-tuple-element.66), channel_id=1, source_target_pairs={{0,24},{1,9},{8,0},{9,17},{16,8},{17,25},{24,16},{25,1},{2,26},{3,... | collective-permute-start | bytes 589832 | tf_op jit(solution)/shard_map/ppermute | solution.py:29
  92.8 19.6 %collective-permute-start.28 = (bf16[16,6144]{1,0:T(8,128)(2,1)}, bf16[16,6144]{1,0:T(8,128)(2,1)S(1)}, u32[]{:S(2)}, u32[]{:S(2)}) collective-permute-start(bf16[16,6144]{1,0:T(8,128)(2,1)} %get-tuple-element.67), channel_id=1, source_target_pairs={{0,8},{1,25},{8,16},{9,1},{16,24},{17,9},{24,0},{25,17},{2,10},{3,... | collective-permute-start | bytes 589832 | tf_op jit(solution)/shard_map/ppermute | solution.py:29
  97.1 24.6 %collective-permute-start.25 = (bf16[16,6144]{1,0:T(8,128)(2,1)S(1)}, bf16[16,6144]{1,0:T(8,128)(2,1)S(1)}, u32[]{:S(2)}, u32[]{:S(2)}) collective-permute-start(bf16[16,6144]{1,0:T(8,128)(2,1)S(1)} %get-tuple-element.77), channel_id=1, source_target_pairs={{0,6},{1,3},{2,0},{3,5},{4,2},{5,7},{6,4},{7,1},{8,14},{9,11},{10,... | collective-permute-start | bytes 589832 | tf_op jit(solution)/shard_map/ppermute | solution.py:29
  105.8 16.0 %collective-permute-start.30 = (bf16[16,6144]{1,0:T(8,128)(2,1)S(1)}, bf16[16,6144]{1,0:T(8,128)(2,1)S(1)}, u32[]{:S(2)}, u32[]{:S(2)}) collective-permute-start(bf16[16,6144]{1,0:T(8,128)(2,1)S(1)} %get-tuple-element.76), channel_id=1, source_target_pairs={{0,4},{2,6},{4,0},{6,2},{1,5},{3,7},{5,1},{7,3},{8,12},{10,14},{12... | collective-permute-start | bytes 589832 | tf_op jit(solution)/shard_map/ppermute | solution.py:20
  110.3 11.4 %collective-permute-start.19 = (bf16[16,6144]{1,0:T(8,128)(2,1)S(1)}, bf16[16,6144]{1,0:T(8,128)(2,1)S(1)}, u32[]{:S(2)}, u32[]{:S(2)}) collective-permute-start(bf16[16,6144]{1,0:T(8,128)(2,1)S(1)} %copy-done.16), channel_id=1, source_target_pairs={{0,24},{1,9},{8,0},{9,17},{16,8},{17,25},{24,16},{25,1},{2,26},{3,... | collective-permute-start | bytes 589832 | tf_op jit(solution)/shard_map/ppermute | solution.py:29
  (26 other events, 434.7 us)

commit v3 on v2

--- a/solution.py
+++ b/solution.py
@@ -224,10 +224,6 @@
     return block, behind, ahead, lane.ring(behind, axis, 1)
 
 
-def joined(mine, passing):
-    return (mine + passing.astype(F32)).astype(BF16)
-
-
 def place_kernel(ids_ref, share_ref, stay_ref, *refs):
     *got, out_ref = refs
     onehot, first, second = chosen(ids_ref[...])
@@ -300,7 +296,7 @@
     behind_x = gather_ring(over_x, behind, "x")
     far_x = gather_ring(over_x, far, "x")
     weights = (up, up_other, down, down_other)
-    near = expert((*own_x, *behind_x, *far_x), weights, ((1, 2), (0,)), (BF16, F32), 1024, 2048)
+    near = expert((*own_x, *behind_x, *far_x), weights, ((1, 2), (0,)), (BF16, BF16), 1024, 2048)
     step = lead * outer_keys + after(summed, near[0])
     new_outer = outer_keys - OUTER_RATE * step
     share = lax.dynamic_slice_in_dim(step, place_at * width, width, 1)
@@ -315,13 +311,12 @@
     pair = keep_p + sum(part.astype(F32) for part in after_all(sent, keep_a))
     last_sent = [hop(far_a, "x", 2), mirrored(prev_a, "x", -1), mirrored(next_a, "x", 1)]
     last = keep_a + sum(part.astype(F32) for part in last_sent)
-    far_o, prev_o = after_all((far_o, prev_o), far_a)
-    own_pass, own_got = mirrored(far_o, "x", 1), mirrored(prev_o, "x", -1)
-    own_end = mirrored(joined(next_o, own_pass), "x", 1)
+    far_o, prev_o, next_o = after_all((far_o, prev_o, next_o), far_a)
+    own_sent = [hop(far_o, "x", 2), mirrored(prev_o, "x", -1), mirrored(next_o, "x", 1)]
     from_far = hop(pair[CAP:].astype(BF16), "zh", 2)
     from_ahead = mirrored(pair[:CAP].astype(BF16), "zh", -1)
     from_behind = mirrored(last.astype(BF16), "zh", 1)
-    input_grad = place(ids, gate_share, keep_o, own_got, own_end, from_ahead, from_behind, from_far)
+    input_grad = place(ids, gate_share, keep_o, *own_sent, from_ahead, from_behind, from_far)
     return input_grad[None], new_outer, new_momentum, new_outer.astype(BF16)
 
 

time: 128 us -> 132 us (1.031); the launches traced: 125 us -> 132 us
  starting transfers between devices: 64.8 us -> 68.4 us
  waiting for transfers between devices: 21.6 us -> 24.9 us
    ppermute x23 -> x22, waiting for transfers between devices: 21.5 us -> 24.9 us  [mirrored(): return lax.ppermute(value, (axis, 'core'), pairs)]
    ppermute x23 -> x22, starting transfers between devices: 46.1 us -> 48.2 us  [mirrored(): return lax.ppermute(value, (axis, 'core'), pairs)]
    ppermute x6 -> x7, starting transfers between devices: 11.3 us -> 12.7 us  [hop(): lax.ppermute(value, axis, [(i, (i + step) % size) for i in range(size)])]
  transfers between devices with their start and end apart: 32 -> 32, of which waited for: 9 -> 8; matrix products, arithmetic and copies ran while one was open for 8% -> 7% of each run, Pallas kernels for 19% -> 18%
where the time goes in v3:
time: 132 us
  starting transfers between devices  68.4 us (52%)
  Pallas kernels  26.5 us (20%)
  waiting for transfers between devices  24.9 us (19%)
  other arithmetic  6.19 us (5%)
  local copies, waits for them, and re-layouts  4.95 us (4%)
    ppermute x22, starting transfers between devices, mirrored(): return lax.ppermute(value, (axis, 'core'), pairs)  48.2 us
    ppermute x22, waiting for transfers between devices, mirrored(): return lax.ppermute(value, (axis, 'core'), pairs)  24.9 us
    pallas_call x2, Pallas kernels, expert(): pl.pallas_call(functools.partial(expert_kernel, rings, chunk, wide), out_...  20.3 us
    ppermute x7, starting transfers between devices, hop(): lax.ppermute(value, axis, [(i, (i + step) % size) for i in range(size)])  12.7 us
    ppermute x3, starting transfers between devices, swap(): return lax.ppermute(value, (axis, 'core'), pairs)  7.46 us
    unnamed x39, local copies, waits for them, and re-layouts  4.92 us
    pallas_call x1, Pallas kernels, pick(): pl.pallas_call(pick_kernel, out_shape=jax.ShapeDtypeStruct((2 * CAP, widt...  3.54 us
    pallas_call x1, Pallas kernels, place(): pl.pallas_call(place_kernel, grid=(3,), out_shape=jax.ShapeDtypeStruct((c...  2.69 us
  transfers between devices with their start and end apart: 32, of which 8 were waited for; matrix products, arithmetic and copies ran while one was open for 7% of the time, Pallas kernels for 18%

profile of v3, /device:TPU:6, one launch (start us, length us, event | category | flops | bytes accessed | tf_op | source)
XLA Modules:
  0.0 131.8 jit_solution(1089965388390628936)
XLA Ops:
  1.2 3.5 %pick.1.refs_0_ = bf16[32,6144]{1,0:T(8,128)(2,1)} custom-call(s32[2,128]{1,0:T(2,128)} %bitcast.14, bf16[128,6144]{1,0:T(8,128)(2,1)} %bitcast.23, bf16[128,6144]{1,0:T(8,128)(2,1)} %bitcast.24), custom_call_target="tpu_custom_call" | custom-call | flops 50331648 | bytes 3145728 | tf_op jit(solution)/shard_map/pick/pallas_call | solution.py:80
  4.8 2.3 %collective-permute-start = (bf16[32,6144]{1,0:T(8,128)(2,1)}, bf16[32,6144]{1,0:T(8,128)(2,1)}, u32[]{:S(2)}, u32[]{:S(2)}) collective-permute-start(bf16[32,6144]{1,0:T(8,128)(2,1)} %pick.1.refs_0_), channel_id=1, source_target_pairs={{0,8},{1,25},{8,16},{9,1},{16,24},{17,9},{24,0},{25,17},{2,10},{3,... | collective-permute-start | bytes 1179656 | tf_op jit(solution)/shard_map/ppermute | solution.py:29
  10.2 2.8 %collective-permute-done.refs_1_ = bf16[32,6144]{1,0:T(8,128)(2,1)} collective-permute-done((bf16[32,6144]{1,0:T(8,128)(2,1)}, bf16[32,6144]{1,0:T(8,128)(2,1)}, u32[]{:S(2)}, u32[]{:S(2)}) %collective-permute-start) | collective-permute-done | bytes 393248 | tf_op jit(solution)/shard_map/ppermute | solution.py:29
  13.0 3.4 %collective-permute-start.2 = (bf16[32,6144]{1,0:T(8,128)(2,1)}, bf16[32,6144]{1,0:T(8,128)(2,1)}, u32[]{:S(2)}, u32[]{:S(2)}) collective-permute-start(bf16[32,6144]{1,0:T(8,128)(2,1)} %collective-permute-done.refs_1_), channel_id=1, source_target_pairs={{0,8},{1,25},{8,16},{9,1},{16,24},{17,9},{24,0},{25,17},{2,10},{3,... | collective-permute-start | bytes 1179656 | tf_op jit(solution)/shard_map/ppermute | solution.py:29
  19.3 3.5 %collective-permute-start.9 = (bf16[32,6144]{1,0:T(8,128)(2,1)}, bf16[32,6144]{1,0:T(8,128)(2,1)}, u32[]{:S(2)}, u32[]{:S(2)}) collective-permute-start(bf16[32,6144]{1,0:T(8,128)(2,1)} %collective-permute-done.3.refs_4_), channel_id=1, source_target_pairs={{0,2},{1,7},{2,4},{3,1},{4,6},{5,3},{6,0},{7,5},{8,10},{9,15},{10,... | collective-permute-start | bytes 1179656 | tf_op jit(solution)/shard_map/ppermute | solution.py:29
  28.7 5.3 %collective-permute-done.5.refs_5_ = bf16[32,6144]{1,0:T(8,128)(2,1)} collective-permute-done((bf16[32,6144]{1,0:T(8,128)(2,1)}, bf16[32,6144]{1,0:T(8,128)(2,1)}, u32[]{:S(2)}, u32[]{:S(2)}) %collective-permute-start.5) | collective-permute-done | bytes 393248 | tf_op jit(solution)/shard_map/ppermute | solution.py:29
  35.4 2.0 %collective-permute-done.7.refs_6_ = bf16[32,6144]{1,0:T(8,128)(2,1)} collective-permute-done((bf16[32,6144]{1,0:T(8,128)(2,1)}, bf16[32,6144]{1,0:T(8,128)(2,1)}, u32[]{:S(2)}, u32[]{:S(2)}) %collective-permute-start.7) | collective-permute-done | bytes 393248 | tf_op jit(solution)/shard_map/ppermute | solution.py:29
  38.7 3.1 %collective-permute-start.15 = (f32[192,512]{0,1:T(8,128)S(1)}, f32[192,512]{0,1:T(8,128)S(1)}, u32[]{:S(2)}, u32[]{:S(2)}) collective-permute-start(f32[192,512]{0,1:T(8,128)S(1)} %add.46), channel_id=1, source_target_pairs={{0,96},{1,33},{32,64},{33,1},{64,32},{65,97},{96,0},{97,65},{2,98}... | collective-permute-start | bytes 1179656 | tf_op jit(solution)/shard_map/ppermute | solution.py:260
  41.8 4.6 %collective-permute-start.14 = (bf16[32,6144]{1,0:T(8,128)(2,1)S(1)}, bf16[32,6144]{1,0:T(8,128)(2,1)}, u32[]{:S(2)}, u32[]{:S(2)}) collective-permute-start(bf16[32,6144]{1,0:T(8,128)(2,1)S(1)} %copy-done.6), channel_id=1, source_target_pairs={{0,6},{1,3},{2,0},{3,5},{4,2},{5,7},{6,4},{7,1},{8,14},{9,11},{10,... | collective-permute-start | bytes 1179656 | tf_op jit(solution)/shard_map/ppermute | solution.py:29
  46.4 3.2 %collective-permute-start.13 = (bf16[32,6144]{1,0:T(8,128)(2,1)S(1)}, bf16[32,6144]{1,0:T(8,128)(2,1)S(1)}, u32[]{:S(2)}, u32[]{:S(2)}) collective-permute-start(bf16[32,6144]{1,0:T(8,128)(2,1)S(1)} %collective-permute-done.10.refs_9_), channel_id=1, source_target_pairs={{0,8},{1,25},{8,16},{9,1},{16,24},{17,9},{24,0},{25,17},{2,10},{3,... | collective-permute-start | bytes 1179656 | tf_op jit(solution)/shard_map/ppermute | solution.py:29
  49.7 2.7 %collective-permute-start.31 = (f32[192,512]{0,1:T(8,128)S(1)}, f32[192,512]{0,1:T(8,128)}, u32[]{:S(2)}, u32[]{:S(2)}) collective-permute-start(f32[192,512]{0,1:T(8,128)S(1)} %add.53), channel_id=1, source_target_pairs={{0,128},{1,129},{128,0},{129,1},{2,130},{3,131},{130,2},{131,3},{4... | collective-permute-start | bytes 1179656 | tf_op jit(solution)/shard_map/ppermute | solution.py:260
  54.1 2.5 %collective-permute-start.16 = (bf16[32,6144]{1,0:T(8,128)(2,1)}, bf16[32,6144]{1,0:T(8,128)(2,1)S(1)}, u32[]{:S(2)}, u32[]{:S(2)}) collective-permute-start(bf16[32,6144]{1,0:T(8,128)(2,1)} %collective-permute-done.14.refs_0_), channel_id=1, source_target_pairs={{0,8},{1,25},{8,16},{9,1},{16,24},{17,9},{24,0},{25,17},{2,10},{3,... | collective-permute-start | bytes 1179656 | tf_op jit(solution)/shard_map/ppermute | solution.py:29
  59.2 3.8 %collective-permute-start.18 = (bf16[32,6144]{1,0:T(8,128)(2,1)}, bf16[32,6144]{1,0:T(8,128)(2,1)}, u32[]{:S(2)}, u32[]{:S(2)}) collective-permute-start(bf16[32,6144]{1,0:T(8,128)(2,1)} %collective-permute-done.14.refs_0_), channel_id=1, source_target_pairs={{0,16},{8,24},{16,0},{24,8},{1,17},{9,25},{17,1},{25,9},{2,18},{10... | collective-permute-start | bytes 1179656 | tf_op jit(solution)/shard_map/ppermute | solution.py:20
  62.9 10.9 %expert.2 = (f32[32,6144]{1,0:T(8,128)}, bf16[32,6144]{1,0:T(8,128)(2,1)}, bf16[32,6144]{1,0:T(8,128)(2,1)}, bf16[32,6144]{1,0:T(8,128)(2,1)}, f32[16,6144]{1,0:...) custom-call(bf16[32,6144]{1,0:T(8,128)(2,1)} %pick.1.refs_0_, ...), custom_call_target="tpu_custom_call" | custom-call | flops 3623878656 | bytes 25165824 | tf_op jit(solution)/shard_map/expert/pallas_call | solution.py:171
  80.8 9.4 %expert.3 = (f32[16,6144]{1,0:T(8,128)}, bf16[16,6144]{1,0:T(8,128)(2,1)}, bf16[16,6144]{1,0:T(8,128)(2,1)}, bf16[16,6144]{1,0:T(8,128)(2,1)}) custom-call(bf16[32,6144]{1,0:T(8,128)(2,1)} %collective-permute-done.14.refs_0_, bf16[32,6144]{1,0:T(8,128)(2,1)} %copy-done.8, bf16[32,6144]{1,0:T(8,128)(2,1)} %collective-permute-done.17.refs_2_, ...), custom_call_target="tpu_custom_call" | custom-call | flops 1207959552 | bytes 25165824 | tf_op jit(solution)/shard_map/expert/pallas_call | solution.py:171
  90.3 2.3 %collective-permute-start.26 = (bf16[16,6144]{1,0:T(8,128)(2,1)}, bf16[16,6144]{1,0:T(8,128)(2,1)S(1)}, u32[]{:S(2)}, u32[]{:S(2)}) collective-permute-start(bf16[16,6144]{1,0:T(8,128)(2,1)} %get-tuple-element.56), channel_id=1, source_target_pairs={{0,16},{8,24},{16,0},{24,8},{1,17},{9,25},{17,1},{25,9},{2,18},{10... | collective-permute-start | bytes 589832 | tf_op jit(solution)/shard_map/ppermute | solution.py:20
  92.8 3.1 %collective-permute-start.28 = (bf16[16,6144]{1,0:T(8,128)(2,1)}, bf16[16,6144]{1,0:T(8,128)(2,1)S(1)}, u32[]{:S(2)}, u32[]{:S(2)}) collective-permute-start(bf16[16,6144]{1,0:T(8,128)(2,1)} %get-tuple-element.69), channel_id=1, source_target_pairs={{0,8},{1,25},{8,16},{9,1},{16,24},{17,9},{24,0},{25,17},{2,10},{3,... | collective-permute-start | bytes 589832 | tf_op jit(solution)/shard_map/ppermute | solution.py:29
  97.1 8.7 %collective-permute-start.25 = (bf16[16,6144]{1,0:T(8,128)(2,1)S(1)}, bf16[16,6144]{1,0:T(8,128)(2,1)S(1)}, u32[]{:S(2)}, u32[]{:S(2)}) collective-permute-start(bf16[16,6144]{1,0:T(8,128)(2,1)S(1)} %get-tuple-element.79), channel_id=1, source_target_pairs={{0,6},{1,3},{2,0},{3,5},{4,2},{5,7},{6,4},{7,1},{8,14},{9,11},{10,... | collective-permute-start | bytes 589832 | tf_op jit(solution)/shard_map/ppermute | solution.py:29
  105.8 4.5 %collective-permute-start.30 = (bf16[16,6144]{1,0:T(8,128)(2,1)S(1)}, bf16[16,6144]{1,0:T(8,128)(2,1)S(1)}, u32[]{:S(2)}, u32[]{:S(2)}) collective-permute-start(bf16[16,6144]{1,0:T(8,128)(2,1)S(1)} %get-tuple-element.78), channel_id=1, source_target_pairs={{0,4},{2,6},{4,0},{6,2},{1,5},{3,7},{5,1},{7,3},{8,12},{10,14},{12... | collective-permute-start | bytes 589832 | tf_op jit(solution)/shard_map/ppermute | solution.py:20
  111.8 3.2 %collective-permute-start.21 = (bf16[16,6144]{1,0:T(8,128)(2,1)S(1)}, bf16[16,6144]{1,0:T(8,128)(2,1)S(1)}, u32[]{:S(2)}, u32[]{:S(2)}) collective-permute-start(bf16[16,6144]{1,0:T(8,128)(2,1)S(1)} %copy-done.15), channel_id=1, source_target_pairs={{0,8},{1,25},{8,16},{9,1},{16,24},{17,9},{24,0},{25,17},{2,10},{3,... | collective-permute-start | bytes 589832 | tf_op jit(solution)/shard_map/ppermute | solution.py:29
  115.1 5.4 %collective-permute-done.25.refs_3_ = bf16[16,6144]{1,0:T(8,128)(2,1)S(1)} collective-permute-done((bf16[16,6144]{1,0:T(8,128)(2,1)S(1)}, bf16[16,6144]{1,0:T(8,128)(2,1)S(1)}, u32[]{:S(2)}, u32[]{:S(2)}) %collective-permute-start.25) | collective-permute-done | bytes 196640 | tf_op jit(solution)/shard_map/ppermute | solution.py:29
  120.5 2.3 %collective-permute-start.29 = (bf16[16,6144]{1,0:T(8,128)(2,1)S(1)}, bf16[16,6144]{1,0:T(8,128)(2,1)S(1)}, u32[]{:S(2)}, u32[]{:S(2)}) collective-permute-start(bf16[16,6144]{1,0:T(8,128)(2,1)S(1)} %add_convert_fusion.1), channel_id=1, source_target_pairs={{0,2},{1,7},{2,4},{3,1},{4,6},{5,3},{6,0},{7,5},{8,10},{9,15},{10,... | collective-permute-start | bytes 589832 | tf_op jit(solution)/shard_map/ppermute | solution.py:29
  123.4 5.7 %collective-permute-done.29.refs_4_ = bf16[16,6144]{1,0:T(8,128)(2,1)S(1)} collective-permute-done((bf16[16,6144]{1,0:T(8,128)(2,1)S(1)}, bf16[16,6144]{1,0:T(8,128)(2,1)S(1)}, u32[]{:S(2)}, u32[]{:S(2)}) %collective-permute-start.29) | collective-permute-done | bytes 196640 | tf_op jit(solution)/shard_map/ppermute | solution.py:29
  129.2 2.7 %place.1 = bf16[128,6144]{1,0:T(8,128)(2,1)} custom-call(s32[2,128]{1,0:T(2,128)S(1)} %bitcast.15, f32[1,128]{1,0:T(1,128)S(1)} %copy-done.2, f32[16,6144]{1,0:T(8,128)S(1)} %copy-done, bf16[16,6144]{1,0:T(8,128)(2,1)S(1)} %collective-permute-done.19.refs_0_, bf16[16,6144]{1,0:T(8,128)(2,1)S(1)} %collective-permute-done.20.refs_1_, ...), custom_call_target="tpu_custom_call" | custom-call | flops 25165824 | bytes 1572864 | tf_op jit(solution)/shard_map/place/pallas_call | solution.py:244
  (95 shorter events, 30.0 us)
Async XLA Ops:
  0.6 22.2 %collective-permute-start.4 = (bf16[6144,256]{1,0:T(8,128)(2,1)}, bf16[6144,256]{1,0:T(8,128)(2,1)S(1)}, u32[]{:S(2)}, u32[]{:S(2)}) collective-permute-start(bf16[6144,256]{1,0:T(8,128)(2,1)} %bitcast.16), channel_id=1, source_target_pairs={{0,1},{1,0},{2,3},{3,2},{4,5},{5,4},{6,7},{7,6},{8,9},{9,8},{10,11... | collective-permute-start | bytes 9437192 | tf_op jit(solution)/shard_map/ppermute | solution.py:20
  0.7 23.7 %collective-permute-start.6 = (bf16[256,6144]{1,0:T(8,128)(2,1)}, bf16[256,6144]{1,0:T(8,128)(2,1)}, u32[]{:S(2)}, u32[]{:S(2)}) collective-permute-start(bf16[256,6144]{1,0:T(8,128)(2,1)} %bitcast.19), channel_id=1, source_target_pairs={{0,1},{1,0},{2,3},{3,2},{4,5},{5,4},{6,7},{7,6},{8,9},{9,8},{10,11... | collective-permute-start | bytes 9437192 | tf_op jit(solution)/shard_map/ppermute | solution.py:20
  7.1 12.2 %collective-permute-start.3 = (bf16[32,6144]{1,0:T(8,128)(2,1)}, bf16[32,6144]{1,0:T(8,128)(2,1)}, u32[]{:S(2)}, u32[]{:S(2)}) collective-permute-start(bf16[32,6144]{1,0:T(8,128)(2,1)} %pick.1.refs_0_), channel_id=1, source_target_pairs={{0,2},{1,7},{2,4},{3,1},{4,6},{5,3},{6,0},{7,5},{8,10},{9,15},{10,... | collective-permute-start | bytes 1179656 | tf_op jit(solution)/shard_map/ppermute | solution.py:29
  8.6 14.2 %collective-permute-start.1 = (bf16[32,6144]{1,0:T(8,128)(2,1)}, bf16[32,6144]{1,0:T(8,128)(2,1)}, u32[]{:S(2)}, u32[]{:S(2)}) collective-permute-start(bf16[32,6144]{1,0:T(8,128)(2,1)} %pick.1.refs_0_), channel_id=1, source_target_pairs={{0,24},{1,9},{8,0},{9,17},{16,8},{17,25},{24,16},{25,1},{2,26},{3,... | collective-permute-start | bytes 1179656 | tf_op jit(solution)/shard_map/ppermute | solution.py:29
  19.3 16.1 %collective-permute-start.9 = (bf16[32,6144]{1,0:T(8,128)(2,1)}, bf16[32,6144]{1,0:T(8,128)(2,1)}, u32[]{:S(2)}, u32[]{:S(2)}) collective-permute-start(bf16[32,6144]{1,0:T(8,128)(2,1)} %collective-permute-done.3.refs_4_), channel_id=1, source_target_pairs={{0,2},{1,7},{2,4},{3,1},{4,6},{5,3},{6,0},{7,5},{8,10},{9,15},{10,... | collective-permute-start | bytes 1179656 | tf_op jit(solution)/shard_map/ppermute | solution.py:29
  24.4 13.0 %collective-permute-start.7 = (bf16[32,6144]{1,0:T(8,128)(2,1)}, bf16[32,6144]{1,0:T(8,128)(2,1)}, u32[]{:S(2)}, u32[]{:S(2)}) collective-permute-start(bf16[32,6144]{1,0:T(8,128)(2,1)} %collective-permute-done.3.refs_4_), channel_id=1, source_target_pairs={{0,24},{1,9},{8,0},{9,17},{16,8},{17,25},{24,16},{25,1},{2,26},{3,... | collective-permute-start | bytes 1179656 | tf_op jit(solution)/shard_map/ppermute | solution.py:29
  27.0 11.7 %collective-permute-start.11 = (f32[192,512]{0,1:T(8,128)S(1)}, f32[192,512]{0,1:T(8,128)S(1)}, u32[]{:S(2)}, u32[]{:S(2)}) collective-permute-start(f32[192,512]{0,1:T(8,128)S(1)} %bitcast_subtract_fusion), channel_id=1, source_target_pairs={{0,32},{1,97},{32,0},{33,65},{64,96},{65,33},{96,64},{97,1},{2,34}... | collective-permute-start | bytes 1179656 | tf_op jit(solution)/shard_map/ppermute | solution.py:260
  33.9 12.5 %collective-permute-start.8 = (bf16[32,6144]{1,0:T(8,128)(2,1)}, bf16[32,6144]{1,0:T(8,128)(2,1)S(1)}, u32[]{:S(2)}, u32[]{:S(2)}) collective-permute-start(bf16[32,6144]{1,0:T(8,128)(2,1)} %collective-permute-done.5.refs_5_), channel_id=1, source_target_pairs={{0,8},{1,25},{8,16},{9,1},{16,24},{17,9},{24,0},{25,17},{2,10},{3,... | collective-permute-start | bytes 1179656 | tf_op jit(solution)/shard_map/ppermute | solution.py:29
  41.8 12.3 %collective-permute-start.14 = (bf16[32,6144]{1,0:T(8,128)(2,1)S(1)}, bf16[32,6144]{1,0:T(8,128)(2,1)}, u32[]{:S(2)}, u32[]{:S(2)}) collective-permute-start(bf16[32,6144]{1,0:T(8,128)(2,1)S(1)} %copy-done.6), channel_id=1, source_target_pairs={{0,6},{1,3},{2,0},{3,5},{4,2},{5,7},{6,4},{7,1},{8,14},{9,11},{10,... | collective-permute-start | bytes 1179656 | tf_op jit(solution)/shard_map/ppermute | solution.py:29
  49.7 24.2 %collective-permute-start.31 = (f32[192,512]{0,1:T(8,128)S(1)}, f32[192,512]{0,1:T(8,128)}, u32[]{:S(2)}, u32[]{:S(2)}) collective-permute-start(f32[192,512]{0,1:T(8,128)S(1)} %add.53), channel_id=1, source_target_pairs={{0,128},{1,129},{128,0},{129,1},{2,130},{3,131},{130,2},{131,3},{4... | collective-permute-start | bytes 1179656 | tf_op jit(solution)/shard_map/ppermute | solution.py:260
  54.1 21.2 %collective-permute-start.16 = (bf16[32,6144]{1,0:T(8,128)(2,1)}, bf16[32,6144]{1,0:T(8,128)(2,1)S(1)}, u32[]{:S(2)}, u32[]{:S(2)}) collective-permute-start(bf16[32,6144]{1,0:T(8,128)(2,1)} %collective-permute-done.14.refs_0_), channel_id=1, source_target_pairs={{0,8},{1,25},{8,16},{9,1},{16,24},{17,9},{24,0},{25,17},{2,10},{3,... | collective-permute-start | bytes 1179656 | tf_op jit(solution)/shard_map/ppermute | solution.py:29
  57.7 23.2 %collective-permute-start.17 = (bf16[32,6144]{1,0:T(8,128)(2,1)}, bf16[32,6144]{1,0:T(8,128)(2,1)}, u32[]{:S(2)}, u32[]{:S(2)}) collective-permute-start(bf16[32,6144]{1,0:T(8,128)(2,1)} %collective-permute-done.14.refs_0_), channel_id=1, source_target_pairs={{0,24},{1,9},{8,0},{9,17},{16,8},{17,25},{24,16},{25,1},{2,26},{3,... | collective-permute-start | bytes 1179656 | tf_op jit(solution)/shard_map/ppermute | solution.py:29
  59.2 21.7 %collective-permute-start.18 = (bf16[32,6144]{1,0:T(8,128)(2,1)}, bf16[32,6144]{1,0:T(8,128)(2,1)}, u32[]{:S(2)}, u32[]{:S(2)}) collective-permute-start(bf16[32,6144]{1,0:T(8,128)(2,1)} %collective-permute-done.14.refs_0_), channel_id=1, source_target_pairs={{0,16},{8,24},{16,0},{24,8},{1,17},{9,25},{17,1},{25,9},{2,18},{10... | collective-permute-start | bytes 1179656 | tf_op jit(solution)/shard_map/ppermute | solution.py:20
  73.9 18.9 %collective-permute-start.22 = (bf16[32,6144]{1,0:T(8,128)(2,1)}, bf16[32,6144]{1,0:T(8,128)(2,1)S(1)}, u32[]{:S(2)}, u32[]{:S(2)}) collective-permute-start(bf16[32,6144]{1,0:T(8,128)(2,1)} %get-tuple-element.61), channel_id=1, source_target_pairs={{0,16},{8,24},{16,0},{24,8},{1,17},{9,25},{17,1},{25,9},{2,18},{10... | collective-permute-start | bytes 1179656 | tf_op jit(solution)/shard_map/ppermute | solution.py:20
  74.0 21.9 %collective-permute-start.23 = (bf16[32,6144]{1,0:T(8,128)(2,1)}, bf16[32,6144]{1,0:T(8,128)(2,1)S(1)}, u32[]{:S(2)}, u32[]{:S(2)}) collective-permute-start(bf16[32,6144]{1,0:T(8,128)(2,1)} %get-tuple-element.62), channel_id=1, source_target_pairs={{0,24},{1,9},{8,0},{9,17},{16,8},{17,25},{24,16},{25,1},{2,26},{3,... | collective-permute-start | bytes 1179656 | tf_op jit(solution)/shard_map/ppermute | solution.py:29
  75.3 20.6 %collective-permute-start.24 = (bf16[32,6144]{1,0:T(8,128)(2,1)}, bf16[32,6144]{1,0:T(8,128)(2,1)}, u32[]{:S(2)}, u32[]{:S(2)}) collective-permute-start(bf16[32,6144]{1,0:T(8,128)(2,1)} %get-tuple-element.63), channel_id=1, source_target_pairs={{0,8},{1,25},{8,16},{9,1},{16,24},{17,9},{24,0},{25,17},{2,10},{3,... | collective-permute-start | bytes 1179656 | tf_op jit(solution)/shard_map/ppermute | solution.py:29
  90.3 20.0 %collective-permute-start.26 = (bf16[16,6144]{1,0:T(8,128)(2,1)}, bf16[16,6144]{1,0:T(8,128)(2,1)S(1)}, u32[]{:S(2)}, u32[]{:S(2)}) collective-permute-start(bf16[16,6144]{1,0:T(8,128)(2,1)} %get-tuple-element.56), channel_id=1, source_target_pairs={{0,16},{8,24},{16,0},{24,8},{1,17},{9,25},{17,1},{25,9},{2,18},{10... | collective-permute-start | bytes 589832 | tf_op jit(solution)/shard_map/ppermute | solution.py:20
  92.6 19.1 %collective-permute-start.27 = (bf16[16,6144]{1,0:T(8,128)(2,1)}, bf16[16,6144]{1,0:T(8,128)(2,1)S(1)}, u32[]{:S(2)}, u32[]{:S(2)}) collective-permute-start(bf16[16,6144]{1,0:T(8,128)(2,1)} %get-tuple-element.68), channel_id=1, source_target_pairs={{0,24},{1,9},{8,0},{9,17},{16,8},{17,25},{24,16},{25,1},{2,26},{3,... | collective-permute-start | bytes 589832 | tf_op jit(solution)/shard_map/ppermute | solution.py:29
  92.8 19.0 %collective-permute-start.28 = (bf16[16,6144]{1,0:T(8,128)(2,1)}, bf16[16,6144]{1,0:T(8,128)(2,1)S(1)}, u32[]{:S(2)}, u32[]{:S(2)}) collective-permute-start(bf16[16,6144]{1,0:T(8,128)(2,1)} %get-tuple-element.69), channel_id=1, source_target_pairs={{0,8},{1,25},{8,16},{9,1},{16,24},{17,9},{24,0},{25,17},{2,10},{3,... | collective-permute-start | bytes 589832 | tf_op jit(solution)/shard_map/ppermute | solution.py:29
  97.1 23.4 %collective-permute-start.25 = (bf16[16,6144]{1,0:T(8,128)(2,1)S(1)}, bf16[16,6144]{1,0:T(8,128)(2,1)S(1)}, u32[]{:S(2)}, u32[]{:S(2)}) collective-permute-start(bf16[16,6144]{1,0:T(8,128)(2,1)S(1)} %get-tuple-element.79), channel_id=1, source_target_pairs={{0,6},{1,3},{2,0},{3,5},{4,2},{5,7},{6,4},{7,1},{8,14},{9,11},{10,... | collective-permute-start | bytes 589832 | tf_op jit(solution)/shard_map/ppermute | solution.py:29
  105.8 17.6 %collective-permute-start.30 = (bf16[16,6144]{1,0:T(8,128)(2,1)S(1)}, bf16[16,6144]{1,0:T(8,128)(2,1)S(1)}, u32[]{:S(2)}, u32[]{:S(2)}) collective-permute-start(bf16[16,6144]{1,0:T(8,128)(2,1)S(1)} %get-tuple-element.78), channel_id=1, source_target_pairs={{0,4},{2,6},{4,0},{6,2},{1,5},{3,7},{5,1},{7,3},{8,12},{10,14},{12... | collective-permute-start | bytes 589832 | tf_op jit(solution)/shard_map/ppermute | solution.py:20
  110.3 13.1 %collective-permute-start.19 = (bf16[16,6144]{1,0:T(8,128)(2,1)S(1)}, bf16[16,6144]{1,0:T(8,128)(2,1)S(1)}, u32[]{:S(2)}, u32[]{:S(2)}) collective-permute-start(bf16[16,6144]{1,0:T(8,128)(2,1)S(1)} %copy-done.17), channel_id=1, source_target_pairs={{0,16},{8,24},{16,0},{24,8},{1,17},{9,25},{17,1},{25,9},{2,18},{10... | collective-permute-start | bytes 589832 | tf_op jit(solution)/shard_map/ppermute | solution.py:20
  111.8 11.6 %collective-permute-start.20 = (bf16[16,6144]{1,0:T(8,128)(2,1)S(1)}, bf16[16,6144]{1,0:T(8,128)(2,1)S(1)}, u32[]{:S(2)}, u32[]{:S(2)}) collective-permute-start(bf16[16,6144]{1,0:T(8,128)(2,1)S(1)} %copy-done.16), channel_id=1, source_target_pairs={{0,24},{1,9},{8,0},{9,17},{16,8},{17,25},{24,16},{25,1},{2,26},{3,... | collective-permute-start | bytes 589832 | tf_op jit(solution)/shard_map/ppermute | solution.py:29
  111.8 11.6 %collective-permute-start.21 = (bf16[16,6144]{1,0:T(8,128)(2,1)S(1)}, bf16[16,6144]{1,0:T(8,128)(2,1)S(1)}, u32[]{:S(2)}, u32[]{:S(2)}) collective-permute-start(bf16[16,6144]{1,0:T(8,128)(2,1)S(1)} %copy-done.15), channel_id=1, source_target_pairs={{0,8},{1,25},{8,16},{9,1},{16,24},{17,9},{24,0},{25,17},{2,10},{3,... | collective-permute-start | bytes 589832 | tf_op jit(solution)/shard_map/ppermute | solution.py:29
  (26 other events, 470.2 us)
